TPU v7x, 32 devices: a whole 2x2x4 slice. The times are simulated.
32 devices in a mesh: grp: 4 (over x, core), seq: 8 (over z, y).
Axes of the slice: x: 2, y: 2, z: 4, core: 2. Of those that a mesh axis runs over, the one named last changes fastest.
Arguments:
- queries: bfloat16 [4096, 4096], P(('grp', 'seq')), may hold values from -6 to 6
- kv_pairs: bfloat16 [2, 4096, 256], P(None, ('grp', 'seq')), may hold values from -6 to 6
- residual: bfloat16 [4096, 4096], P(('grp', 'seq')), may hold values from -30 to 30
- norm_gain: bfloat16 [4096], replicated, may hold values from 0.099609375 to 1.8984375
- o_weight: bfloat16 [4096, 4096], P('seq'), may hold values from -0.09375 to 0.09375
- w_in: bfloat16 [32, 4096, 1536], P(('grp', 'seq')), may hold values from -0.09375 to 0.09375
- w_down: bfloat16 [32, 768, 4096], P(('grp', 'seq')), may hold values from -0.21875 to 0.21875
- expert_ids: int32 [4096, 4], P(('grp', 'seq')), may hold values from 0 to 31, all different within a row; in each aligned block of 128 rows (0 to 127, 128 to 255, ...) at most 32 rows name the same one
- route_weights: float32 [4096, 4], P(('grp', 'seq')), may hold values from 0.1 to 0.6
Outputs:
- layer_out: bfloat16 [4096, 4096], P(('grp', 'seq'))
Inputs may be any that keep to these rules, and one draw needn't show every extreme that they name: `expert_ids`: within the rows of one device (aligned blocks of 128 rows) no expert is named by more than 32 rows, a bound that some block reaches; each row names 4 different experts, and every expert is named somewhere.
All inputs are finite; a program needn't handle non-finite values.
Results may differ from a plain program's by a relative error of at most 0.01.
Values may be sent and summed in bfloat16 or wider, within the bound.
A program may use at most 128 MiB of HBM per device.

v0:
```python
import jax
import jax.numpy as jnp
from jax import lax
from jax.sharding import PartitionSpec as P

HD = 128


def shards(
    queries, kv_pairs, residual, norm_gain, o_weight, w_in, w_down, expert_ids, route_weights
):
    tok_dev = queries.shape[0]
    width = residual.shape[1]
    n_seq = lax.axis_size("seq")
    n_grp = lax.axis_size("grp")
    devices = n_seq * n_grp
    head_size = HD
    heads_all = queries.shape[1] // head_size
    per_device = heads_all // n_seq
    key_heads = kv_pairs.shape[2] // head_size
    sharing = heads_all // key_heads
    head_queries = lax.all_to_all(queries, "seq", split_axis=1, concat_axis=0, tiled=True)
    seq_len = head_queries.shape[0]
    kv_all = lax.all_gather(kv_pairs, "seq", axis=1, tiled=True)
    first_col = lax.axis_index("seq") * per_device // sharing * head_size
    kv_mine = lax.dynamic_slice_in_dim(kv_all, first_col, head_size, 2)
    key_rows = kv_mine[0]
    value_rows = kv_mine[1]
    block = min(512, seq_len)
    num_blocks = seq_len // block
    query_blocks = head_queries.reshape(num_blocks, block, per_device, head_size)
    key_positions = jnp.arange(seq_len, dtype=jnp.int32)
    scale = 1.0 / head_size**0.5

    def attend(operands):
        query_block, block_index = operands
        scores = (
            jnp.einsum("qhd,kd->hqk", query_block, key_rows, preferred_element_type=jnp.float32)
            * scale
        )
        query_positions = block_index * block + jnp.arange(block, dtype=jnp.int32)
        allowed = key_positions[None, :] <= query_positions[:, None]
        scores = jnp.where(allowed[None], scores, jnp.float32(-1e30))
        top_score = jnp.max(scores, axis=2, keepdims=True)
        weights = jnp.exp(scores - top_score)
        probs = (weights / jnp.sum(weights, axis=2, keepdims=True)).astype(jnp.bfloat16)
        result = jnp.einsum("hqk,kd->qhd", probs, value_rows, preferred_element_type=jnp.float32)
        return result.astype(jnp.bfloat16).reshape(block, per_device * head_size)

    attended = lax.map(attend, (query_blocks, jnp.arange(num_blocks, dtype=jnp.int32)))
    attended = attended.reshape(seq_len, per_device * head_size)
    attn_out = lax.psum_scatter(
        jnp.dot(attended, o_weight, preferred_element_type=jnp.float32).astype(jnp.bfloat16),
        "seq",
        scatter_dimension=0,
        tiled=True,
    ).astype(jnp.float32)
    mixed = residual.astype(jnp.float32) + attn_out
    mean_square = jnp.mean(mixed * mixed, axis=1, keepdims=True)
    normed = (mixed * lax.rsqrt(mean_square + 1e-06) * norm_gain.astype(jnp.float32)).astype(
        jnp.bfloat16
    )
    top_count = expert_ids.shape[1]
    capacity = 2 * tok_dev * top_count // devices
    flat_ids = expert_ids.reshape(-1)
    flat_weights = route_weights.reshape(-1)
    onehot = (flat_ids[:, None] == jnp.arange(devices, dtype=jnp.int32)[None, :]).astype(jnp.int32)
    earlier = jnp.cumsum(onehot, axis=0) - onehot
    rank = jnp.sum(earlier * onehot, axis=1)
    slot_index = flat_ids * capacity + rank
    source_rows = jnp.arange(flat_ids.shape[0], dtype=jnp.int32) // top_count
    outgoing_rows = (
        jnp.zeros((devices * capacity, width), jnp.bfloat16).at[slot_index].set(normed[source_rows])
    )
    outgoing_rows = outgoing_rows.reshape(devices, capacity, width)
    ffe_width = w_down.shape[1]
    arrived = lax.all_to_all(outgoing_rows, ("grp", "seq"), split_axis=0, concat_axis=0, tiled=True)
    flat_rows = arrived.reshape(-1, width)
    projected = jnp.dot(flat_rows, w_in[0], preferred_element_type=jnp.float32)
    hidden = (jax.nn.silu(projected[:, :ffe_width]) * projected[:, ffe_width:]).astype(jnp.bfloat16)
    produced = jnp.dot(hidden, w_down[0], preferred_element_type=jnp.float32).astype(jnp.bfloat16)
    returned = lax.all_to_all(
        produced.reshape(arrived.shape), ("grp", "seq"), split_axis=0, concat_axis=0, tiled=True
    )
    returned = returned.reshape(devices * capacity, width)
    picked = returned[slot_index].astype(jnp.float32) * flat_weights[:, None]
    combined = jnp.sum(picked.reshape(tok_dev, top_count, width), axis=1)
    return (mixed + combined).astype(jnp.bfloat16)


def solution(mesh):
    return jax.shard_map(
        shards,
        mesh=mesh,
        in_specs=(
            P(("grp", "seq"), None),
            P(None, ("grp", "seq"), None),
            P(("grp", "seq"), None),
            P(),
            P("seq", None),
            P(("grp", "seq"), None, None),
            P(("grp", "seq"), None, None),
            P(("grp", "seq"), None),
            P(("grp", "seq"), None),
        ),
        out_specs=P(("grp", "seq"), None),
        check_vma=False,
    )
```

profile of v0, /device:TPU:0, one launch (start us, length us, event | category | flops | bytes accessed | tf_op | source)
XLA Modules:
  0.0 714.8 jit_solution(12902524603638471049)
XLA Ops:
  6.5 0.7 all-gather.2.cloned.1.call-update
  7.3 2.4 copy.39
  9.6 7.3 %all-to-all-start = ((bf16[128,8,512]{2,0,1:T(8,128)(2,1)}), bf16[128,8,512]{2,0,1:T(8,128)(2,1)S(1)}, u32[]{:S(2)}, u32[]{:S(2)}) async-start(bf16[128,8,512]{2,0,1:T(8,128)(2,1)} %bitcast.85), calls=%async_computation | async-start | bytes 2097152 | tf_op jit(solution)/shard_map/all_to_all | solution.py:22
  17.0 41.4 %all-gather.2.cloned.1.call-done = bf16[2,1024,256]{2,1,0:T(8,128)(2,1)} async-done(((bf16[2,128,256]{2,1,0:T(8,128)(2,1)}), bf16[2,1024,256]{2,1,0:T(8,128)(2,1)}) %all-gather.2.cloned.1.call-update) | async-done | bytes 1048592 | tf_op jit(solution)/shard_map/all_gather | solution.py:24
  58.4 1.1 dynamic-slice_bitcast_fusion
  59.9 26.7 %while.11 = (s32[]{:T(128)}, bf16[2,512,512]{2,1,0:T(8,128)(2,1)}, s32[2]{0:T(128)S(1)}, bf16[2,512,4,128]{3,2,1,0:T(4,128)(2,1)S(1)}, bf16[1024,128]{1,0:T(8,12...) while((s32[]{:T(128)}, bf16[2,512,512]{2,1,0:T(8,128)(2,1)}, ...), condition=%wide.region_3.4_spmd.clone, body=%wide.region_0.3_spmd.clone.sunk | while | flops 1087112704 | bytes 22565492 | solution.py:50
  59.9 0.7 dynamic_slice.18
  61.3 0.4 iota_compare_fusion.4
  61.9 5.4 fusion.49
  67.2 5.0 fusion.50
  72.4 0.8 constant_dynamic-update-slice_fusion.2
  73.3 0.7 dynamic_slice.18
  75.2 5.4 fusion.49
  80.6 5.0 fusion.50
  85.8 0.8 constant_dynamic-update-slice_fusion.2
  86.6 10.2 %convolution_convert_fusion.1 = bf16[1024,4096]{1,0:T(8,128)(2,1)} fusion(bf16[1024,512]{1,0:T(8,128)(2,1)} %bitcast.110, bf16[512,4096]{1,0:T(8,128)(2,1)} %param.15), kind=kOutput, calls=%fused_computation.32 | convolution fusion | flops 4299161600 | bytes 13631488 | tf_op jit(solution)/shard_map/dot_general | solution.py:53
  96.9 0.7 copy-done.3
  97.9 1.2 reduce-window.6
  99.7 145.1 %reduce-scatter.2.cloned.1.call-done = bf16[128,4096]{1,0:T(8,128)(2,1)} async-done(((bf16[1024,4096]{1,0:T(8,128)(2,1)}), bf16[128,4096]{1,0:T(8,128)(2,1)}) %reduce-scatter.2.cloned.1.call-update) | async-done | bytes 1048592 | tf_op jit(solution)/shard_map/reduce_scatter | solution.py:52
  244.8 1.6 multiply_reduce_fusion.1
  246.5 1.6 multiply_convert_fusion
  248.1 4.4 gather_fusion
  252.4 12.6 %scatter_custom_fusion = bf16[1024,4096]{1,0:T(8,128)(2,1)} fusion(s32[512]{0:T(512)S(1)} %bitcast.104, bf16[512,4096]{1,0:T(8,128)(2,1)} %gather_fusion, bf16[]{:T(256)} %constant.67.clone.1), kind=kCustom, calls=%fused_computation.34 | custom fusion | bytes 8389120 | tf_op jit(solution)/shard_map/scatter | solution.py:73
  265.1 188.7 %all_to_all.26 = bf16[32,32,4096]{2,1,0:T(8,128)(2,1)S(1)} all-to-all(bf16[32,32,4096]{2,1,0:T(8,128)(2,1)} %bitcast.98), channel_id=1, replica_groups=mesh['grp'=4,'seq'=8] {'grp','seq'}, dimensions={0} | all-to-all | bytes 16777216 | tf_op jit(solution)/shard_map/all_to_all | solution.py:77
  453.7 15.8 %fusion.22 = f32[1024,1536]{1,0:T(8,128)S(1)} fusion(bf16[1024,4096]{1,0:T(8,128)(2,1)S(1)} %bitcast.101, bf16[1,4096,1536]{2,1,0:T(8,128)(2,1)} %param.16), kind=kOutput, calls=%fused_computation.28 | convolution fusion | flops 12884901888 | bytes 27262976 | tf_op jit(solution)/shard_map/dot_general | solution.py:79
  469.6 8.9 %convolution_convert_fusion = bf16[1024,4096]{1,0:T(8,128)(2,1)} fusion(bf16[1,768,4096]{2,1,0:T(8,128)(2,1)S(1)} %bitcast.109, f32[1024,1536]{1,0:T(8,128)S(1)} %fusion.22), kind=kOutput, calls=%fused_computation.31 | convolution fusion | flops 6451363840 | bytes 20971520 | tf_op jit(solution)/shard_map/dot_general | solution.py:81
  478.5 3.8 all-to-all-start.2
  482.4 189.3 %all-to-all-done.2 = bf16[32,32,4096]{2,1,0:T(8,128)(2,1)} async-done(((bf16[32,32,4096]{2,1,0:T(8,128)(2,1)}), bf16[32,32,4096]{2,1,0:T(8,128)(2,1)}, u32[]{:S(2)}, u32[]{:S(2)}) %all-to-all-start.2) | async-done | bytes 8388640 | tf_op jit(solution)/shard_map/all_to_all | solution.py:82
  671.8 13.0 %gather_fusion.1 = bf16[512,4096]{1,0:T(8,128)(2,1)} fusion(bf16[1024,4096]{1,0:T(8,128)(2,1)} %bitcast.13, s32[1024]{0:T(1024)S(1)} %pad_clamp_fusion), kind=kCustom, calls=%fused_computation.1 | custom fusion | bytes 8390656 | tf_op jit(solution)/shard_map/gather | solution.py:86
  684.8 8.5 %reshape.175 = f32[128,4,4096]{2,1,0:T(4,128)} reshape(bf16[512,4096]{1,0:T(8,128)(2,1)} %gather_fusion.1) | data formatting | bytes 12582912 | tf_op jit(solution)/shard_map/convert_element_type | solution.py:86
  693.3 11.2 %multiply_reduce_fusion = f32[128,4096]{1,0:T(8,128)} fusion(f32[128,4,4096]{2,1,0:T(4,128)} %reshape.175, f32[128,4]{1,0:T(8,128)S(1)} %copy.20), kind=kLoop, calls=%fused_computation.30 | loop fusion | flops 3670016 | bytes 10487808 | tf_op jit(solution)/shard_map/reduce_sum | solution.py:87
  704.6 2.9 add_convert_fusion
  (47 shorter events, 2.8 us)
Async XLA Ops:
  6.5 51.8 %all-gather.2.cloned.1.call-start = ((), (), s32[]{:S(2)}) async-start(), calls=%async_computation.4 | async-start | bytes 1179648 | tf_op jit(solution)/shard_map/all_gather | solution.py:24
  9.6 50.0 %all-to-all-start = ((bf16[128,8,512]{2,0,1:T(8,128)(2,1)}), bf16[128,8,512]{2,0,1:T(8,128)(2,1)S(1)}, u32[]{:S(2)}, u32[]{:S(2)}) async-start(bf16[128,8,512]{2,0,1:T(8,128)(2,1)} %bitcast.85), calls=%async_computation | async-start | bytes 2097152 | tf_op jit(solution)/shard_map/all_to_all | solution.py:22
  16.9 227.9 %reduce-scatter.2.cloned.1.call-start = ((), (), s32[]{:S(2)}) async-start(), calls=%async_computation.5 | async-start | bytes 9437184 | tf_op jit(solution)/shard_map/reduce_scatter | solution.py:52
  96.8 0.7 copy-start.3
  96.9 1.0 copy-start.2
  96.9 147.9 %copy-start = (bf16[128,4096]{1,0:T(8,128)(2,1)S(1)}, bf16[128,4096]{1,0:T(8,128)(2,1)}, u32[]{:S(2)}) copy-start(bf16[128,4096]{1,0:T(8,128)(2,1)} %param.13) | copy-start | bytes 3145732
  265.1 204.5 %slice-start = ((s8[6291456]{0:T(1024)(128)(4,1)}), s8[4194304]{0:T(1024)(128)(4,1)S(1)}, s32[]{:S(2)}) async-start(s8[6291456]{0:T(1024)(128)(4,1)} %bitcast.108), calls=%async_computation.6 | async-start | bytes 8388608
  453.7 15.8 %slice-start.1 = ((s8[6291456]{0:T(1024)(128)(4,1)}), s8[2097152]{0:T(1024)(128)(4,1)S(1)}, s32[]{:S(2)}) async-start(s8[6291456]{0:T(1024)(128)(4,1)} %bitcast.108), calls=%async_computation.7 | async-start | bytes 4194304
  478.5 3.8 copy-start.4
  478.5 193.3 %all-to-all-start.2 = ((bf16[32,32,4096]{2,1,0:T(8,128)(2,1)}), bf16[32,32,4096]{2,1,0:T(8,128)(2,1)}, u32[]{:S(2)}, u32[]{:S(2)}) async-start(bf16[32,32,4096]{2,1,0:T(8,128)(2,1)} %bitcast.100), calls=%async_computation.3 | async-start | bytes 16777216 | tf_op jit(solution)/shard_map/all_to_all | solution.py:82
  693.3 11.2 %copy-start.1 = (bf16[128,4096]{1,0:T(8,128)(2,1)S(1)}, bf16[128,4096]{1,0:T(8,128)(2,1)}, u32[]{:S(2)}) copy-start(bf16[128,4096]{1,0:T(8,128)(2,1)} %reduce-scatter.2.cloned.1.call-done) | copy-start | bytes 3145732
Sparse Core Ops, SparseCore 0:
  9.5 48.7 all-gather.1
  97.0 147.7 reduce-scatter.1
where the time goes:
time: 724 us; the launch traced here: 715 us
  waiting for transfers between devices  377 us (52%)
  blocking collectives  189 us (26%)
  matrix products  55.7 us (8%)
  local copies, waits for them, and re-layouts  47.7 us (7%)
  other arithmetic  19.5 us (3%)
  between operations  14 us (2%)
  starting transfers between devices  11.1 us (2%)
    all_to_all x1, waiting for transfers between devices, shards(): lax.all_to_all(produced.reshape(arrived.shape), ('grp', 'seq'), split_axi...  189 us
    all_to_all x1, blocking collectives, shards(): lax.all_to_all(outgoing_rows, ('grp', 'seq'), split_axis=0, concat_axis=0...  189 us
    reduce_scatter x1, waiting for transfers between devices, shards(): lax.psum_scatter(jnp.dot(attended, o_weight, preferred_element_type=jnp.f...  145 us
    all_gather x1, waiting for transfers between devices, shards(): kv_all = lax.all_gather(kv_pairs, 'seq', axis=1, tiled=True)  41.4 us
    dot_general x1, matrix products, shards(): projected = jnp.dot(flat_rows, w_in[0], preferred_element_type=jnp.float32)  15.8 us
  transfers between devices with their start and end apart: 4, of which 3 were waited for; matrix products, arithmetic and copies ran while one was open for 1% of the time, Pallas kernels for 0%

commit v1 on v0

v1 whole, which is shorter than its diff:
```python
import jax
import jax.numpy as jnp
from jax import lax
from jax.sharding import Mesh, PartitionSpec as P

HD = 128
PLANE = ("x", "core", "y")


def ring(value, axis):
    n = lax.axis_size(axis)
    return lax.ppermute(value, axis, [(i, (i + 1) % n) for i in range(n)])


def spread(value, axes):
    n = 1
    for axis in axes:
        n *= lax.axis_size(axis)
    return lax.all_to_all(
        jnp.broadcast_to(value[None], (n,) + value.shape), axes, split_axis=0, concat_axis=0, tiled=True
    )


def gathered_weight(o_weight):
    core = lax.axis_index("core")
    rows = o_weight.shape[0] // 2
    half = lax.dynamic_slice_in_dim(o_weight, core * rows, rows, 0)
    shards = [o_weight]
    for _ in range(lax.axis_size("y") - 1):
        half = ring(half, "y")
        other = ring(half, "core")
        first = jnp.where(core == 0, half, other)
        second = jnp.where(core == 0, other, half)
        shards.append(jnp.concatenate([first, second], axis=0))
    return shards


def attention(queries, kv_pairs):
    tok = queries.shape[0]
    nz, ny = lax.axis_size("z"), lax.axis_size("y")
    y = lax.axis_index("y")
    heads = queries.shape[1] // HD
    per_z = heads // nz
    key_heads = kv_pairs.shape[2] // HD
    sharing = heads // key_heads
    mine = lax.all_to_all(
        queries.reshape(tok, nz, per_z * HD).transpose(1, 0, 2), "z", split_axis=0, concat_axis=0, tiled=True
    )
    parts = [
        kv_pairs[:, :, (z * per_z // sharing) * HD : (z * per_z // sharing + 1) * HD] for z in range(nz) for _ in range(ny)
    ]
    kv = lax.all_to_all(jnp.stack(parts), ("z", "y"), split_axis=0, concat_axis=0, tiled=True)
    keys = kv[:, 0].reshape(nz * ny * tok, HD)
    values = kv[:, 1].reshape(nz * ny * tok, HD)
    scale = 1.0 / HD**0.5
    blocks = []
    for b in range(nz):
        length = (b + 1) * ny * tok
        q = mine[b].reshape(tok, per_z, HD)
        scores = jnp.einsum("qhd,kd->hqk", q, keys[:length], preferred_element_type=jnp.float32) * scale
        at = (b * ny + y) * tok + jnp.arange(tok, dtype=jnp.int32)
        allowed = jnp.arange(length, dtype=jnp.int32)[None, :] <= at[:, None]
        scores = jnp.where(allowed[None], scores, jnp.float32(-1e30))
        weights = jnp.exp(scores - jnp.max(scores, axis=2, keepdims=True))
        total = jnp.sum(weights, axis=2, keepdims=True)
        out = jnp.einsum(
            "hqk,kd->hqd", weights.astype(jnp.bfloat16), values[:length], preferred_element_type=jnp.float32
        )
        out = (out / total).astype(jnp.bfloat16)
        blocks.append(out.transpose(1, 0, 2).reshape(tok, per_z * HD))
    return jnp.stack(blocks)


def shards(queries, kv_pairs, residual, norm_gain, o_weight, w_in, w_down, expert_ids, route_weights):
    tok, width = residual.shape
    nx, nz, ny = lax.axis_size("x"), lax.axis_size("z"), lax.axis_size("y")
    z, y = lax.axis_index("z"), lax.axis_index("y")
    devices = nx * 2 * nz * ny
    plane = devices // nz
    top_count = expert_ids.shape[1]
    capacity = 2 * tok * top_count // devices
    ffe = w_down.shape[1]

    routing = spread(
        jnp.concatenate([expert_ids.astype(jnp.float32), route_weights], axis=1), ("z",)
    )
    o_shards = gathered_weight(o_weight)
    attended = attention(queries, kv_pairs)

    depth = o_weight.shape[0]
    acc = None
    for t in range(nz):
        rows = lax.dynamic_index_in_dim(attended, (z + 2 * nz - 1 - t) % nz, 0, keepdims=False)
        part = jnp.zeros((tok, width), jnp.float32)
        for s, shard in enumerate(o_shards):
            columns = lax.dynamic_slice_in_dim(rows, (y + ny - s) % ny * depth, depth, 1)
            part = part + jnp.dot(columns, shard, preferred_element_type=jnp.float32)
        if acc is not None:
            part = part + ring(acc, "z").astype(jnp.float32)
        acc = part.astype(jnp.bfloat16) if t < nz - 1 else part
    mixed = residual.astype(jnp.float32) + acc
    mean_square = jnp.mean(mixed * mixed, axis=1, keepdims=True)
    normed = (mixed * lax.rsqrt(mean_square + 1e-06) * norm_gain.astype(jnp.float32)).astype(jnp.bfloat16)

    number = jnp.arange(plane, dtype=jnp.int32)
    experts = ((number // ny) * nz + z) * ny + number % ny
    before = (jnp.arange(tok)[None, :] < jnp.arange(tok)[:, None]).astype(jnp.bfloat16)
    slots = jnp.arange(capacity, dtype=jnp.float32)

    def tables(s):
        table = lax.dynamic_index_in_dim(routing, (z + nz - s) % nz, 0, keepdims=False)
        hits = table[:, :top_count, None] == experts.astype(jnp.float32)[None, None, :]
        chosen = jnp.any(hits, axis=1)
        weight = jnp.sum(jnp.where(hits, table[:, top_count:, None], 0.0), axis=1)
        rank = jnp.dot(before, chosen.astype(jnp.bfloat16), preferred_element_type=jnp.float32)
        place = chosen[:, :, None] & (rank[:, :, None] == slots[None, None, :])
        send = place.astype(jnp.bfloat16).reshape(tok, plane * capacity)
        back = jnp.where(place, weight[:, :, None], 0.0).astype(jnp.bfloat16).reshape(tok, plane * capacity)
        return send, back

    made = [tables(s) for s in range(nz)]
    block = normed
    produced = []
    for s in range(nz):
        rows = lax.dot_general(
            made[s][0], block, (((0,), (0,)), ((), ())), preferred_element_type=jnp.float32
        ).astype(jnp.bfloat16)
        if s < nz - 1:
            block = ring(block, "z")
        rows = lax.all_to_all(
            rows.reshape(plane, capacity, width), PLANE, split_axis=0, concat_axis=0, tiled=True
        ).reshape(plane * capacity, width)
        projected = jnp.dot(rows, w_in[0], preferred_element_type=jnp.float32)
        hidden = (jax.nn.silu(projected[:, :ffe]) * projected[:, ffe:]).astype(jnp.bfloat16)
        produced.append(jnp.dot(hidden, w_down[0], preferred_element_type=jnp.float32).astype(jnp.bfloat16))

    acc = None
    for t in range(nz):
        s = (t + 1) % nz
        back = lax.all_to_all(
            produced[s].reshape(plane, capacity, width), PLANE, split_axis=0, concat_axis=0, tiled=True
        ).reshape(plane * capacity, width)
        part = jnp.dot(made[s][1], back, preferred_element_type=jnp.float32)
        if acc is not None:
            part = part + ring(acc, "z").astype(jnp.float32)
        acc = part.astype(jnp.bfloat16) if t < nz - 1 else part
    return (mixed + acc).astype(jnp.bfloat16)


def solution(mesh):
    nz = 4
    n_grp, n_seq = mesh.shape["grp"], mesh.shape["seq"]
    fine = Mesh(mesh.devices.reshape(n_grp // 2, 2, nz, n_seq // nz), ("x", "core", "z", "y"))
    every = ("x", "core", "z", "y")
    return jax.shard_map(
        shards,
        mesh=fine,
        in_specs=(
            P(every, None),
            P(None, every, None),
            P(every, None),
            P(),
            P(("z", "y"), None),
            P(every, None, None),
            P(every, None, None),
            P(every, None),
            P(every, None),
        ),
        out_specs=P(every, None),
        check_vma=False,
    )
```

time: 724 us -> 434 us (0.60); the launches traced: 715 us -> 433 us
  blocking collectives: 189 us -> 0 us
  waiting for transfers between devices: 377 us -> 268 us
  starting transfers between devices: 11.1 us -> 50.8 us
  matrix products: 55.7 us -> 79.9 us
  local copies, waits for them, and re-layouts: 47.7 us -> 25.5 us
  between operations: 14 us -> 0.73 us
  other arithmetic: 19.5 us -> 7.7 us
    all_to_all x1 -> x0, blocking collectives: 189 us -> none  [shards(): lax.all_to_all(outgoing_rows, ('grp', 'seq'), split_axis=0, concat_axis=0...]
    reduce_scatter x1 -> x0, waiting for transfers between devices: 145 us -> none  [shards(): lax.psum_scatter(jnp.dot(attended, o_weight, preferred_element_type=jnp.f...]
    ppermute x0 -> x11, waiting for transfers between devices: none -> 141 us  [ring(): return lax.ppermute(value, axis, [(i, (i + 1) % n) for i in range(n)])]
    all_to_all x2 -> x11, waiting for transfers between devices: 189 us -> 127 us  [the longest x4 47.7 us: shards(): lax.all_to_all(produced[s].reshape(plane, capacity, width), PLANE, split_...]
    all_gather x1 -> x0, waiting for transfers between devices: 41.4 us -> none  [shards(): kv_all = lax.all_gather(kv_pairs, 'seq', axis=1, tiled=True)]
    all_to_all x2 -> x11, starting transfers between devices: 11.1 us -> 45.6 us  [the longest x4 16.4 us: shards(): lax.all_to_all(rows.reshape(plane, capacity, width), PLANE, split_axis=0,...]
    dot_general x4 -> x32, matrix products: 36 us -> 61.4 us  [the longest x4 27.9 us: shards(): projected = jnp.dot(rows, w_in[0], preferred_element_type=jnp.float32)]
    unnamed x17 -> x54, local copies, waits for them, and re-layouts: 1.05 us -> 19.9 us
  transfers between devices with their start and end apart: 4 -> 22, of which waited for: 3 -> 16; matrix products, arithmetic and copies ran while one was open for 1% -> 19% of each run, Pallas kernels for 0% -> 0%
where the time goes in v1:
time: 434 us; the launch traced here: 433 us
  waiting for transfers between devices  268 us (62%)
  matrix products  79.9 us (18%)
  starting transfers between devices  50.8 us (12%)
  local copies, waits for them, and re-layouts  25.5 us (6%)
  other arithmetic  7.7 us (2%)
    ppermute x11, waiting for transfers between devices, ring(): return lax.ppermute(value, axis, [(i, (i + 1) % n) for i in range(n)])  141 us
    all_to_all x4, waiting for transfers between devices, shards(): lax.all_to_all(produced[s].reshape(plane, capacity, width), PLANE, split_...  47.7 us
    dot_general x4, matrix products, shards(): projected = jnp.dot(rows, w_in[0], preferred_element_type=jnp.float32)  27.9 us
    all_to_all x4, waiting for transfers between devices, shards(): lax.all_to_all(rows.reshape(plane, capacity, width), PLANE, split_axis=0,...  25.1 us
    all_to_all x1, waiting for transfers between devices, attention(): lax.all_to_all(queries.reshape(tok, nz, per_z * HD).transpose(1, 0, 2), '...  24.3 us
    all_to_all x1, waiting for transfers between devices, spread(): lax.all_to_all(jnp.broadcast_to(value[None], (n,) + value.shape), axes, s...  21.8 us
    unnamed x54, local copies, waits for them, and re-layouts  19.9 us
    dot_general x4, matrix products, shards(): jnp.dot(hidden, w_down[0], preferred_element_type=jnp.float32)  18.5 us
  transfers between devices with their start and end apart: 22, of which 16 were waited for; matrix products, arithmetic and copies ran while one was open for 19% of the time, Pallas kernels for 0%

profile of v1, /device:TPU:0, one launch (start us, length us, event | category | flops | bytes accessed | tf_op | source)
XLA Modules:
  0.0 432.7 jit_solution(1903647681334423295)
XLA Ops:
  11.8 7.3 %all-to-all-start = ((bf16[8,2,128,128]{3,2,1,0:T(8,128)(2,1)}), bf16[8,2,128,128]{3,2,1,0:T(8,128)(2,1)S(1)}, u32[]{:S(2)}, u32[]{:S(2)}) async-start(bf16[8,2,128,128]{3,2,1,0:T(8,128)(2,1)} %bitcast_dynamic-update-slice_fusion.3), calls=%async_computation | async-start | bytes 1048576 | tf_op jit(solution)/shard_map/all_to_all | solution.py:52
  25.7 7.9 %all-to-all-done = bf16[8,2,128,128]{3,2,1,0:T(8,128)(2,1)S(1)} async-done(((bf16[8,2,128,128]{3,2,1,0:T(8,128)(2,1)}), bf16[8,2,128,128]{3,2,1,0:T(8,128)(2,1)S(1)}, u32[]{:S(2)}, u32[]{:S(2)}) %all-to-all-start) | async-done | bytes 524320 | tf_op jit(solution)/shard_map/all_to_all | solution.py:52
  33.5 3.5 all-to-all-start.1
  37.4 24.3 %all-to-all-done.1 = bf16[4,128,1024]{1,2,0:T(8,128)(2,1)S(1)} async-done(((bf16[4,128,1024]{1,2,0:T(8,128)(2,1)}), bf16[4,128,1024]{1,2,0:T(8,128)(2,1)S(1)}, u32[]{:S(2)}, u32[]{:S(2)}) %all-to-all-start.1) | async-done | bytes 1048608 | tf_op jit(solution)/shard_map/all_to_all | solution.py:46
  64.8 8.0 %collective-permute-done = bf16[256,4096]{1,0:T(8,128)(2,1)} collective-permute-done((bf16[256,4096]{1,0:T(8,128)(2,1)}, bf16[256,4096]{1,0:T(8,128)(2,1)}, u32[]{:S(2)}, u32[]{:S(2)}) %collective-permute-start) | collective-permute-done | bytes 2097184 | tf_op jit(solution)/shard_map/ppermute | solution.py:12
  84.9 3.2 all-to-all-start.2
  88.4 21.8 %all-to-all-done.2 = f32[4,128,8]{1,2,0:T(8,128)S(1)} async-done(((f32[4,128,8]{1,2,0:T(8,128)}), f32[4,128,8]{1,2,0:T(8,128)S(1)}, u32[]{:S(2)}, u32[]{:S(2)}) %all-to-all-start.2) | async-done | bytes 16416 | tf_op jit(solution)/shard_map/all_to_all | solution.py:19
  117.3 25.4 %collective-permute-done.3 = bf16[128,4096]{1,0:T(8,128)(2,1)S(1)} collective-permute-done((bf16[128,4096]{1,0:T(8,128)(2,1)S(1)}, bf16[128,4096]{1,0:T(8,128)(2,1)S(1)}, u32[]{:S(2)}, u32[]{:S(2)}) %collective-permute-start.3) | collective-permute-done | bytes 1048608 | tf_op jit(solution)/shard_map/ppermute | solution.py:12
  145.0 24.7 %collective-permute-done.4 = bf16[128,4096]{1,0:T(8,128)(2,1)S(1)} collective-permute-done((bf16[128,4096]{1,0:T(8,128)(2,1)S(1)}, bf16[128,4096]{1,0:T(8,128)(2,1)S(1)}, u32[]{:S(2)}, u32[]{:S(2)}) %collective-permute-start.4) | collective-permute-done | bytes 1048608 | tf_op jit(solution)/shard_map/ppermute | solution.py:12
  173.2 3.6 all-to-all-start.3
  176.9 27.2 %collective-permute-done.5 = bf16[128,4096]{1,0:T(8,128)(2,1)S(1)} collective-permute-done((bf16[128,4096]{1,0:T(8,128)(2,1)S(1)}, bf16[128,4096]{1,0:T(8,128)(2,1)S(1)}, u32[]{:S(2)}, u32[]{:S(2)}) %collective-permute-start.5) | collective-permute-done | bytes 1048608 | tf_op jit(solution)/shard_map/ppermute | solution.py:12
  208.4 4.4 %all-to-all-start.9 = ((bf16[8,32,4096]{2,1,0:T(8,128)(2,1)}), bf16[8,32,4096]{2,1,0:T(8,128)(2,1)}, u32[]{:S(2)}, u32[]{:S(2)}) async-start(bf16[8,32,4096]{2,1,0:T(8,128)(2,1)} %bitcast.74), calls=%async_computation.9 | async-start | bytes 4194304 | tf_op jit(solution)/shard_map/all_to_all | solution.py:130
  212.8 27.2 %collective-permute-done.6 = bf16[128,4096]{1,0:T(8,128)(2,1)S(1)} collective-permute-done((bf16[128,4096]{1,0:T(8,128)(2,1)S(1)}, bf16[128,4096]{1,0:T(8,128)(2,1)S(1)}, u32[]{:S(2)}, u32[]{:S(2)}) %collective-permute-start.6) | collective-permute-done | bytes 1048608 | tf_op jit(solution)/shard_map/ppermute | solution.py:12
  242.1 3.9 all-to-all-start.7
  246.0 7.0 %fusion = f32[256,1536]{1,0:T(8,128)S(1)} fusion(bf16[256,4096]{1,0:T(8,128)(2,1)} %bitcast.75, bf16[1,4096,1536]{2,1,0:T(8,128)(2,1)} %param.14), kind=kOutput, calls=%fused_computation | convolution fusion | flops 3221225472 | bytes 16252928 | tf_op jit(solution)/shard_map/dot_general | solution.py:133
  253.0 6.1 %fusion.25 = bf16[256,4096]{1,0:T(8,128)(2,1)} fusion(bf16[1,768,4096]{2,1,0:T(8,128)(2,1)} %param.15, f32[256,1536]{1,0:T(8,128)S(1)} %fusion), kind=kOutput, calls=%fused_computation.23 | convolution fusion | flops 1612840960 | bytes 9961472 | tf_op jit(solution)/shard_map/dot_general | solution.py:135
  259.1 12.7 %all-to-all-done.7 = bf16[8,32,4096]{2,1,0:T(8,128)(2,1)S(1)} async-done(((bf16[8,32,4096]{2,1,0:T(8,128)(2,1)}), bf16[8,32,4096]{2,1,0:T(8,128)(2,1)S(1)}, u32[]{:S(2)}, u32[]{:S(2)}) %all-to-all-start.7) | async-done | bytes 2097184 | tf_op jit(solution)/shard_map/all_to_all | solution.py:130
  273.1 3.6 all-to-all-start.10
  276.8 27.2 %collective-permute-done.7 = bf16[128,4096]{1,0:T(8,128)(2,1)S(1)} collective-permute-done((bf16[128,4096]{1,0:T(8,128)(2,1)S(1)}, bf16[128,4096]{1,0:T(8,128)(2,1)S(1)}, u32[]{:S(2)}, u32[]{:S(2)}) %collective-permute-start.7) | collective-permute-done | bytes 1048608 | tf_op jit(solution)/shard_map/ppermute | solution.py:12
  307.5 4.6 %all-to-all-start.5 = ((bf16[8,32,4096]{2,1,0:T(8,128)(2,1)}), bf16[8,32,4096]{2,1,0:T(8,128)(2,1)}, u32[]{:S(2)}, u32[]{:S(2)}) async-start(bf16[8,32,4096]{2,1,0:T(8,128)(2,1)} %bitcast.258), calls=%async_computation.5 | async-start | bytes 4194304 | tf_op jit(solution)/shard_map/all_to_all | solution.py:130
  312.1 7.0 %fusion.2 = f32[256,1536]{1,0:T(8,128)S(1)} fusion(bf16[256,4096]{1,0:T(8,128)(2,1)} %bitcast.260, bf16[1,4096,1536]{2,1,0:T(8,128)(2,1)} %param.14), kind=kOutput, calls=%fused_computation.2 | convolution fusion | flops 3221225472 | bytes 16252928 | tf_op jit(solution)/shard_map/dot_general | solution.py:133
  319.2 6.0 %fusion.22 = bf16[256,4096]{1,0:T(8,128)(2,1)} fusion(bf16[1,768,4096]{2,1,0:T(8,128)(2,1)} %param.15, f32[256,1536]{1,0:T(8,128)S(1)} %fusion.2), kind=kOutput, calls=%fused_computation.22 | convolution fusion | flops 1612840960 | bytes 9961472 | tf_op jit(solution)/shard_map/dot_general | solution.py:135
  325.2 12.4 %all-to-all-done.5 = bf16[8,32,4096]{2,1,0:T(8,128)(2,1)} async-done(((bf16[8,32,4096]{2,1,0:T(8,128)(2,1)}), bf16[8,32,4096]{2,1,0:T(8,128)(2,1)}, u32[]{:S(2)}, u32[]{:S(2)}) %all-to-all-start.5) | async-done | bytes 2097184 | tf_op jit(solution)/shard_map/all_to_all | solution.py:130
  337.6 3.6 all-to-all-start.8
  344.4 7.2 %fusion.4 = f32[256,1536]{1,0:T(8,128)S(1)} fusion(bf16[256,4096]{1,0:T(8,128)(2,1)} %bitcast.61, bf16[1,4096,1536]{2,1,0:T(8,128)(2,1)} %param.14), kind=kOutput, calls=%fused_computation.4 | convolution fusion | flops 3221225472 | bytes 16252928 | tf_op jit(solution)/shard_map/dot_general | solution.py:133
  351.7 3.2 fusion.19
  354.9 12.0 %all-to-all-done.8 = bf16[8,32,4096]{2,1,0:T(8,128)(2,1)S(1)} async-done(((bf16[8,32,4096]{2,1,0:T(8,128)(2,1)}), bf16[8,32,4096]{2,1,0:T(8,128)(2,1)S(1)}, u32[]{:S(2)}, u32[]{:S(2)}) %all-to-all-start.8) | async-done | bytes 2097184 | tf_op jit(solution)/shard_map/all_to_all | solution.py:140
  368.3 3.6 all-to-all-start.6
  375.5 6.6 %fusion.6 = f32[256,1536]{1,0:T(8,128)S(1)} fusion(bf16[256,4096]{1,0:T(8,128)(2,1)S(1)} %bitcast.259, bf16[1,4096,1536]{2,1,0:T(8,128)(2,1)} %param.14), kind=kOutput, calls=%fused_computation.6 | convolution fusion | flops 3221225472 | bytes 16252928 | tf_op jit(solution)/shard_map/dot_general | solution.py:133
  385.4 12.3 %all-to-all-done.6 = bf16[8,32,4096]{2,1,0:T(8,128)(2,1)S(1)} async-done(((bf16[8,32,4096]{2,1,0:T(8,128)(2,1)}), bf16[8,32,4096]{2,1,0:T(8,128)(2,1)S(1)}, u32[]{:S(2)}, u32[]{:S(2)}) %all-to-all-start.6) | async-done | bytes 2097184 | tf_op jit(solution)/shard_map/all_to_all | solution.py:140
  397.6 4.4 %all-to-all-start.4 = ((bf16[8,32,4096]{2,1,0:T(8,128)(2,1)}), bf16[8,32,4096]{2,1,0:T(8,128)(2,1)}, u32[]{:S(2)}, u32[]{:S(2)}) async-start(bf16[8,32,4096]{2,1,0:T(8,128)(2,1)} %bitcast.262), calls=%async_computation.4 | async-start | bytes 4194304 | tf_op jit(solution)/shard_map/all_to_all | solution.py:140
  404.4 23.3 %all-to-all-done.4 = bf16[8,32,4096]{2,1,0:T(8,128)(2,1)} async-done(((bf16[8,32,4096]{2,1,0:T(8,128)(2,1)}), bf16[8,32,4096]{2,1,0:T(8,128)(2,1)}, u32[]{:S(2)}, u32[]{:S(2)}) %all-to-all-start.4) | async-done | bytes 2097184 | tf_op jit(solution)/shard_map/all_to_all | solution.py:140
  (142 shorter events, 76.8 us)
Async XLA Ops:
  11.8 21.8 %all-to-all-start = ((bf16[8,2,128,128]{3,2,1,0:T(8,128)(2,1)}), bf16[8,2,128,128]{3,2,1,0:T(8,128)(2,1)S(1)}, u32[]{:S(2)}, u32[]{:S(2)}) async-start(bf16[8,2,128,128]{3,2,1,0:T(8,128)(2,1)} %bitcast_dynamic-update-slice_fusion.3), calls=%async_computation | async-start | bytes 1048576 | tf_op jit(solution)/shard_map/all_to_all | solution.py:52
  19.0 5.3 %copy-start.14 = (bf16[128,4096]{1,0:T(8,128)(2,1)S(1)}, bf16[128,4096]{1,0:T(8,128)(2,1)}, u32[]{:S(2)}) copy-start(bf16[128,4096]{1,0:T(8,128)(2,1)} %param.9) | copy-start | bytes 3145732
  22.3 50.5 %collective-permute-start = (bf16[256,4096]{1,0:T(8,128)(2,1)}, bf16[256,4096]{1,0:T(8,128)(2,1)}, u32[]{:S(2)}, u32[]{:S(2)}) collective-permute-start(bf16[256,4096]{1,0:T(8,128)(2,1)} %constant_dynamic-slice_fusion), channel_id=1, source_target_pairs={{0,1},{1,0},{2,3},{3,2},{4,5},{5,4},{6,7},{7,6},{8,9},{9,8},{10,11... | collective-permute-start | bytes 6291464 | tf_op jit(solution)/shard_map/ppermute | solution.py:12
  33.5 28.2 %all-to-all-start.1 = ((bf16[4,128,1024]{1,2,0:T(8,128)(2,1)}), bf16[4,128,1024]{1,2,0:T(8,128)(2,1)S(1)}, u32[]{:S(2)}, u32[]{:S(2)}) async-start(bf16[4,128,1024]{1,2,0:T(8,128)(2,1)} %bitcast.5), calls=%async_computation.1 | async-start | bytes 2097152 | tf_op jit(solution)/shard_map/all_to_all | solution.py:46
  72.8 5.8 %collective-permute-start.1 = (bf16[256,4096]{1,0:T(8,128)(2,1)}, bf16[256,4096]{1,0:T(8,128)(2,1)S(1)}, u32[]{:S(2)}, u32[]{:S(2)}) collective-permute-start(bf16[256,4096]{1,0:T(8,128)(2,1)} %collective-permute-done), channel_id=1, source_target_pairs={{0,8},{8,0},{1,9},{9,1},{2,10},{10,2},{3,11},{11,3},{4,12},{12,4},... | collective-permute-start | bytes 6291464 | tf_op jit(solution)/shard_map/ppermute | solution.py:12
  80.4 3.9 copy-start.17
  80.4 3.9 copy-start.18
  80.5 7.8 %copy-start.16 = (bf16[4096]{0:T(1024)(128)(2,1)S(1)}, bf16[4096]{0:T(1024)(128)(2,1)}, u32[]{:S(2)}) copy-start(bf16[4096]{0:T(1024)(128)(2,1)} %param.12) | copy-start | bytes 24580
  82.2 31.0 %collective-permute-start.2 = (bf16[128,4096]{1,0:T(8,128)(2,1)}, bf16[128,4096]{1,0:T(8,128)(2,1)}, u32[]{:S(2)}, u32[]{:S(2)}) collective-permute-start(bf16[128,4096]{1,0:T(8,128)(2,1)} %fusion.34), channel_id=1, source_target_pairs={{0,2},{2,4},{4,6},{6,0},{1,3},{3,5},{5,7},{7,1},{8,10},{10,12},{12... | collective-permute-start | bytes 3145736 | tf_op jit(solution)/shard_map/ppermute | solution.py:12
  84.9 25.2 %all-to-all-start.2 = ((f32[4,128,8]{1,2,0:T(8,128)}), f32[4,128,8]{1,2,0:T(8,128)S(1)}, u32[]{:S(2)}, u32[]{:S(2)}) async-start(f32[4,128,8]{1,2,0:T(8,128)} %broadcast_in_dim.174), calls=%async_computation.2 | async-start | bytes 32768 | tf_op jit(solution)/shard_map/all_to_all | solution.py:19
  115.5 27.1 %collective-permute-start.3 = (bf16[128,4096]{1,0:T(8,128)(2,1)S(1)}, bf16[128,4096]{1,0:T(8,128)(2,1)S(1)}, u32[]{:S(2)}, u32[]{:S(2)}) collective-permute-start(bf16[128,4096]{1,0:T(8,128)(2,1)S(1)} %fusion.33), channel_id=1, source_target_pairs={{0,2},{2,4},{4,6},{6,0},{1,3},{3,5},{5,7},{7,1},{8,10},{10,12},{12... | collective-permute-start | bytes 3145736 | tf_op jit(solution)/shard_map/ppermute | solution.py:12
  143.5 26.1 %collective-permute-start.4 = (bf16[128,4096]{1,0:T(8,128)(2,1)S(1)}, bf16[128,4096]{1,0:T(8,128)(2,1)S(1)}, u32[]{:S(2)}, u32[]{:S(2)}) collective-permute-start(bf16[128,4096]{1,0:T(8,128)(2,1)S(1)} %fusion.32), channel_id=1, source_target_pairs={{0,2},{2,4},{4,6},{6,0},{1,3},{3,5},{5,7},{7,1},{8,10},{10,12},{12... | collective-permute-start | bytes 3145736 | tf_op jit(solution)/shard_map/ppermute | solution.py:12
  144.2 25.4 %copy-start.15 = (bf16[128,4096]{1,0:T(8,128)(2,1)S(1)}, bf16[128,4096]{1,0:T(8,128)(2,1)}, u32[]{:S(2)}) copy-start(bf16[128,4096]{1,0:T(8,128)(2,1)} %param.11) | copy-start | bytes 3145732
  173.2 33.9 %all-to-all-start.3 = ((bf16[8,32,4096]{2,1,0:T(8,128)(2,1)}), bf16[8,32,4096]{2,1,0:T(8,128)(2,1)S(1)}, u32[]{:S(2)}, u32[]{:S(2)}) async-start(bf16[8,32,4096]{2,1,0:T(8,128)(2,1)} %bitcast.51), calls=%async_computation.3 | async-start | bytes 4194304 | tf_op jit(solution)/shard_map/all_to_all | solution.py:130
  176.8 27.3 %collective-permute-start.5 = (bf16[128,4096]{1,0:T(8,128)(2,1)S(1)}, bf16[128,4096]{1,0:T(8,128)(2,1)S(1)}, u32[]{:S(2)}, u32[]{:S(2)}) collective-permute-start(bf16[128,4096]{1,0:T(8,128)(2,1)S(1)} %multiply_convert_fusion), channel_id=1, source_target_pairs={{0,2},{2,4},{4,6},{6,0},{1,3},{3,5},{5,7},{7,1},{8,10},{10,12},{12... | collective-permute-start | bytes 3145736 | tf_op jit(solution)/shard_map/ppermute | solution.py:12
  207.1 5.7 %copy-start.13 = (bf16[128,4096]{1,0:T(8,128)(2,1)S(1)}, bf16[128,4096]{1,0:T(8,128)(2,1)}, u32[]{:S(2)}) copy-start(bf16[128,4096]{1,0:T(8,128)(2,1)} %copy-done.12) | copy-start | bytes 3145732
  208.4 33.7 %all-to-all-start.9 = ((bf16[8,32,4096]{2,1,0:T(8,128)(2,1)}), bf16[8,32,4096]{2,1,0:T(8,128)(2,1)}, u32[]{:S(2)}, u32[]{:S(2)}) async-start(bf16[8,32,4096]{2,1,0:T(8,128)(2,1)} %bitcast.74), calls=%async_computation.9 | async-start | bytes 4194304 | tf_op jit(solution)/shard_map/all_to_all | solution.py:130
  212.8 27.2 %collective-permute-start.6 = (bf16[128,4096]{1,0:T(8,128)(2,1)S(1)}, bf16[128,4096]{1,0:T(8,128)(2,1)S(1)}, u32[]{:S(2)}, u32[]{:S(2)}) collective-permute-start(bf16[128,4096]{1,0:T(8,128)(2,1)S(1)} %copy-done.13), channel_id=1, source_target_pairs={{0,2},{2,4},{4,6},{6,0},{1,3},{3,5},{5,7},{7,1},{8,10},{10,12},{12... | collective-permute-start | bytes 3145736 | tf_op jit(solution)/shard_map/ppermute | solution.py:12
  242.1 29.6 %all-to-all-start.7 = ((bf16[8,32,4096]{2,1,0:T(8,128)(2,1)}), bf16[8,32,4096]{2,1,0:T(8,128)(2,1)S(1)}, u32[]{:S(2)}, u32[]{:S(2)}) async-start(bf16[8,32,4096]{2,1,0:T(8,128)(2,1)} %bitcast.67), calls=%async_computation.7 | async-start | bytes 4194304 | tf_op jit(solution)/shard_map/all_to_all | solution.py:130
  273.1 32.9 %all-to-all-start.10 = ((bf16[8,32,4096]{2,1,0:T(8,128)(2,1)}), bf16[8,32,4096]{2,1,0:T(8,128)(2,1)S(1)}, u32[]{:S(2)}, u32[]{:S(2)}) async-start(bf16[8,32,4096]{2,1,0:T(8,128)(2,1)} %bitcast.264), calls=%async_computation.10 | async-start | bytes 4194304 | tf_op jit(solution)/shard_map/all_to_all | solution.py:140
  276.7 27.3 %collective-permute-start.7 = (bf16[128,4096]{1,0:T(8,128)(2,1)S(1)}, bf16[128,4096]{1,0:T(8,128)(2,1)S(1)}, u32[]{:S(2)}, u32[]{:S(2)}) collective-permute-start(bf16[128,4096]{1,0:T(8,128)(2,1)S(1)} %collective-permute-done.6), channel_id=1, source_target_pairs={{0,2},{2,4},{4,6},{6,0},{1,3},{3,5},{5,7},{7,1},{8,10},{10,12},{12... | collective-permute-start | bytes 3145736 | tf_op jit(solution)/shard_map/ppermute | solution.py:12
  307.5 30.2 %all-to-all-start.5 = ((bf16[8,32,4096]{2,1,0:T(8,128)(2,1)}), bf16[8,32,4096]{2,1,0:T(8,128)(2,1)}, u32[]{:S(2)}, u32[]{:S(2)}) async-start(bf16[8,32,4096]{2,1,0:T(8,128)(2,1)} %bitcast.258), calls=%async_computation.5 | async-start | bytes 4194304 | tf_op jit(solution)/shard_map/all_to_all | solution.py:130
  337.6 29.3 %all-to-all-start.8 = ((bf16[8,32,4096]{2,1,0:T(8,128)(2,1)}), bf16[8,32,4096]{2,1,0:T(8,128)(2,1)S(1)}, u32[]{:S(2)}, u32[]{:S(2)}) async-start(bf16[8,32,4096]{2,1,0:T(8,128)(2,1)} %bitcast.263), calls=%async_computation.8 | async-start | bytes 4194304 | tf_op jit(solution)/shard_map/all_to_all | solution.py:140
  341.2 10.4 %slice-start = ((s8[6291456]{0:T(1024)(128)(4,1)}), s8[4194304]{0:T(1024)(128)(4,1)S(1)}, s32[]{:S(2)}) async-start(s8[6291456]{0:T(1024)(128)(4,1)} %bitcast.285), calls=%async_computation.11 | async-start | bytes 8388608
  344.4 27.5 %collective-permute-start.8 = (bf16[128,4096]{1,0:T(8,128)(2,1)}, bf16[128,4096]{1,0:T(8,128)(2,1)S(1)}, u32[]{:S(2)}, u32[]{:S(2)}) collective-permute-start(bf16[128,4096]{1,0:T(8,128)(2,1)} %fusion.35), channel_id=1, source_target_pairs={{0,2},{2,4},{4,6},{6,0},{1,3},{3,5},{5,7},{7,1},{8,10},{10,12},{12... | collective-permute-start | bytes 3145736 | tf_op jit(solution)/shard_map/ppermute | solution.py:12
  344.4 7.2 %slice-start.1 = ((s8[6291456]{0:T(1024)(128)(4,1)}), s8[2097152]{0:T(1024)(128)(4,1)S(1)}, s32[]{:S(2)}) async-start(s8[6291456]{0:T(1024)(128)(4,1)} %bitcast.285), calls=%async_computation.12 | async-start | bytes 4194304
  368.3 29.3 %all-to-all-start.6 = ((bf16[8,32,4096]{2,1,0:T(8,128)(2,1)}), bf16[8,32,4096]{2,1,0:T(8,128)(2,1)S(1)}, u32[]{:S(2)}, u32[]{:S(2)}) async-start(bf16[8,32,4096]{2,1,0:T(8,128)(2,1)} %bitcast.261), calls=%async_computation.6 | async-start | bytes 4194304 | tf_op jit(solution)/shard_map/all_to_all | solution.py:140
  372.9 9.2 %slice-start.2 = ((s8[6291456]{0:T(1024)(128)(4,1)}), s8[4194304]{0:T(1024)(128)(4,1)S(1)}, s32[]{:S(2)}) async-start(s8[6291456]{0:T(1024)(128)(4,1)} %bitcast.287), calls=%async_computation.13 | async-start | bytes 8388608
  375.4 27.4 %collective-permute-start.9 = (bf16[128,4096]{1,0:T(8,128)(2,1)S(1)}, bf16[128,4096]{1,0:T(8,128)(2,1)}, u32[]{:S(2)}, u32[]{:S(2)}) collective-permute-start(bf16[128,4096]{1,0:T(8,128)(2,1)S(1)} %add_convert_fusion.2), channel_id=1, source_target_pairs={{0,2},{2,4},{4,6},{6,0},{1,3},{3,5},{5,7},{7,1},{8,10},{10,12},{12... | collective-permute-start | bytes 3145736 | tf_op jit(solution)/shard_map/ppermute | solution.py:12
  375.5 6.7 %slice-start.3 = ((s8[6291456]{0:T(1024)(128)(4,1)}), s8[2097152]{0:T(1024)(128)(4,1)S(1)}, s32[]{:S(2)}) async-start(s8[6291456]{0:T(1024)(128)(4,1)} %bitcast.287), calls=%async_computation.14 | async-start | bytes 4194304
  397.6 30.2 %all-to-all-start.4 = ((bf16[8,32,4096]{2,1,0:T(8,128)(2,1)}), bf16[8,32,4096]{2,1,0:T(8,128)(2,1)}, u32[]{:S(2)}, u32[]{:S(2)}) async-start(bf16[8,32,4096]{2,1,0:T(8,128)(2,1)} %bitcast.262), calls=%async_computation.4 | async-start | bytes 4194304 | tf_op jit(solution)/shard_map/all_to_all | solution.py:140
  404.4 26.9 %collective-permute-start.10 = (bf16[128,4096]{1,0:T(8,128)(2,1)S(1)}, bf16[128,4096]{1,0:T(8,128)(2,1)S(1)}, u32[]{:S(2)}, u32[]{:S(2)}) collective-permute-start(bf16[128,4096]{1,0:T(8,128)(2,1)S(1)} %add_convert_fusion.1), channel_id=1, source_target_pairs={{0,2},{2,4},{4,6},{6,0},{1,3},{3,5},{5,7},{7,1},{8,10},{10,12},{12... | collective-permute-start | bytes 3145736 | tf_op jit(solution)/shard_map/ppermute | solution.py:12
  (13 other events, 26.1 us)

commit v2 on v1

--- a/solution.py
+++ b/solution.py
@@ -42,14 +42,14 @@
     heads = queries.shape[1] // HD
     per_z = heads // nz
     key_heads = kv_pairs.shape[2] // HD
-    sharing = heads // key_heads
     mine = lax.all_to_all(
         queries.reshape(tok, nz, per_z * HD).transpose(1, 0, 2), "z", split_axis=0, concat_axis=0, tiled=True
     )
-    parts = [
-        kv_pairs[:, :, (z * per_z // sharing) * HD : (z * per_z // sharing + 1) * HD] for z in range(nz) for _ in range(ny)
-    ]
-    kv = lax.all_to_all(jnp.stack(parts), ("z", "y"), split_axis=0, concat_axis=0, tiled=True)
+    split = kv_pairs.reshape(2, tok, key_heads, HD).transpose(2, 0, 1, 3)
+    parts = jnp.broadcast_to(split[:, None], (key_heads, nz * ny // key_heads, 2, tok, HD))
+    kv = lax.all_to_all(
+        parts.reshape(nz * ny, 2, tok, HD), ("z", "y"), split_axis=0, concat_axis=0, tiled=True
+    )
     keys = kv[:, 0].reshape(nz * ny * tok, HD)
     values = kv[:, 1].reshape(nz * ny * tok, HD)
     scale = 1.0 / HD**0.5
@@ -102,8 +102,22 @@
     mean_square = jnp.mean(mixed * mixed, axis=1, keepdims=True)
     normed = (mixed * lax.rsqrt(mean_square + 1e-06) * norm_gain.astype(jnp.float32)).astype(jnp.bfloat16)
 
+    x, core = lax.axis_index("x"), lax.axis_index("core")
     number = jnp.arange(plane, dtype=jnp.int32)
-    experts = ((number // ny) * nz + z) * ny + number % ny
+    peer_x = (x + number // (2 * ny)) % nx
+    peer_core = (core + number // ny % 2) % 2
+    peer_y = (y + number % ny) % ny
+    experts = ((peer_x * 2 + peer_core) * nz + z) * ny + peer_y
+
+    def moves(r, sign):
+        pairs = []
+        for i in range(plane):
+            to_x = (i // (2 * ny) + sign * (r // (2 * ny))) % nx
+            to_core = (i // ny % 2 + sign * (r // ny % 2)) % 2
+            to_y = (i % ny + sign * (r % ny)) % ny
+            pairs.append((i, (to_x * 2 + to_core) * ny + to_y))
+        return pairs
+
     before = (jnp.arange(tok)[None, :] < jnp.arange(tok)[:, None]).astype(jnp.bfloat16)
     slots = jnp.arange(capacity, dtype=jnp.float32)
 
@@ -119,28 +133,32 @@
         return send, back
 
     made = [tables(s) for s in range(nz)]
-    block = normed
-    produced = []
+    def expert(rows):
+        projected = jnp.dot(rows, w_in[0], preferred_element_type=jnp.float32)
+        hidden = (jax.nn.silu(projected[:, :ffe]) * projected[:, ffe:]).astype(jnp.bfloat16)
+        return jnp.dot(hidden, w_down[0], preferred_element_type=jnp.float32).astype(jnp.bfloat16)
+
+    def exchange(rows, sign):
+        parts = []
+        for r in range(plane):
+            part = rows[r * capacity : (r + 1) * capacity]
+            parts.append(part if r == 0 else lax.ppermute(part, PLANE, moves(r, sign)))
+        return jnp.concatenate(parts, axis=0)
+
+    blocks = [normed]
+    for s in range(nz - 1):
+        blocks.append(ring(blocks[-1], "z"))
+    returned = []
     for s in range(nz):
         rows = lax.dot_general(
-            made[s][0], block, (((0,), (0,)), ((), ())), preferred_element_type=jnp.float32
+            made[s][0], blocks[s], (((0,), (0,)), ((), ())), preferred_element_type=jnp.float32
         ).astype(jnp.bfloat16)
-        if s < nz - 1:
-            block = ring(block, "z")
-        rows = lax.all_to_all(
-            rows.reshape(plane, capacity, width), PLANE, split_axis=0, concat_axis=0, tiled=True
-        ).reshape(plane * capacity, width)
-        projected = jnp.dot(rows, w_in[0], preferred_element_type=jnp.float32)
-        hidden = (jax.nn.silu(projected[:, :ffe]) * projected[:, ffe:]).astype(jnp.bfloat16)
-        produced.append(jnp.dot(hidden, w_down[0], preferred_element_type=jnp.float32).astype(jnp.bfloat16))
+        returned.append(exchange(expert(exchange(rows, 1)), -1))
 
     acc = None
     for t in range(nz):
         s = (t + 1) % nz
-        back = lax.all_to_all(
-            produced[s].reshape(plane, capacity, width), PLANE, split_axis=0, concat_axis=0, tiled=True
-        ).reshape(plane * capacity, width)
-        part = jnp.dot(made[s][1], back, preferred_element_type=jnp.float32)
+        part = jnp.dot(made[s][1], returned[s], preferred_element_type=jnp.float32)
         if acc is not None:
             part = part + ring(acc, "z").astype(jnp.float32)
         acc = part.astype(jnp.bfloat16) if t < nz - 1 else part

time: 434 us -> 584 us (1.35); the launches traced: 433 us -> 575 us
  waiting for transfers between devices: 268 us -> 451 us
  matrix products: 79.9 us -> 43.7 us
  local copies, waits for them, and re-layouts: 25.5 us -> 11 us
  starting transfers between devices: 50.8 us -> 63.1 us
    ppermute x0 -> x56, waiting for transfers between devices: none -> 294 us  [exchange(): parts.append(part if r == 0 else lax.ppermute(part, PLANE, moves(r, sign)))]
    all_to_all x9 -> x1, waiting for transfers between devices: 80.7 us -> 7.85 us  [attention(): lax.all_to_all(parts.reshape(nz * ny, 2, tok, HD), ('z', 'y'), split_axis...]
    ppermute x0 -> x56, starting transfers between devices: none -> 43.2 us  [exchange(): parts.append(part if r == 0 else lax.ppermute(part, PLANE, moves(r, sign)))]
    ppermute x11, waiting for transfers between devices: 141 us -> 102 us  [ring(): return lax.ppermute(value, axis, [(i, (i + 1) % n) for i in range(n)])]
    dot_general x16, matrix products: 63 us -> 26.7 us  [the longest x4 13.6 us: expert(): projected = jnp.dot(rows, w_in[0], preferred_element_type=jnp.float32)]
    all_to_all x9 -> x1, starting transfers between devices: 38.9 us -> 7.28 us  [attention(): lax.all_to_all(parts.reshape(nz * ny, 2, tok, HD), ('z', 'y'), split_axis...]
    unnamed x54 -> x77, local copies, waits for them, and re-layouts: 19.9 us -> 3.15 us
  transfers between devices with their start and end apart: 22 -> 70, of which waited for: 16 -> 54; matrix products, arithmetic and copies ran while one was open for 19% -> 7% of each run, Pallas kernels for 0% -> 0%
where the time goes in v2:
time: 584 us; the launch traced here: 575 us
  waiting for transfers between devices  451 us (77%)
  starting transfers between devices  63.1 us (11%)
  matrix products  43.7 us (7%)
  local copies, waits for them, and re-layouts  11 us (2%)
    ppermute x56, waiting for transfers between devices, exchange(): parts.append(part if r == 0 else lax.ppermute(part, PLANE, moves(r, sign)))  294 us
    ppermute x11, waiting for transfers between devices, ring(): return lax.ppermute(value, axis, [(i, (i + 1) % n) for i in range(n)])  102 us
    ppermute x56, starting transfers between devices, exchange(): parts.append(part if r == 0 else lax.ppermute(part, PLANE, moves(r, sign)))  43.2 us
    all_to_all x1, waiting for transfers between devices, attention(): lax.all_to_all(queries.reshape(tok, nz, per_z * HD).transpose(1, 0, 2), '...  24.3 us
    all_to_all x1, waiting for transfers between devices, spread(): lax.all_to_all(jnp.broadcast_to(value[None], (n,) + value.shape), axes, s...  21.8 us
    dot_general x4, matrix products, expert(): projected = jnp.dot(rows, w_in[0], preferred_element_type=jnp.float32)  13.6 us
  transfers between devices with their start and end apart: 70, of which 54 were waited for; matrix products, arithmetic and copies ran while one was open for 7% of the time, Pallas kernels for 0%

profile of v2, /device:TPU:0, one launch (start us, length us, event | category | flops | bytes accessed | tf_op | source)
XLA Modules:
  0.0 575.1 jit_solution(299145718847514859)
XLA Ops:
  1.9 7.3 %all-to-all-start = ((bf16[8,2,128,128]{3,2,1,0:T(8,128)(2,1)}), bf16[8,2,128,128]{3,2,1,0:T(8,128)(2,1)S(1)}, u32[]{:S(2)}, u32[]{:S(2)}) async-start(bf16[8,2,128,128]{3,2,1,0:T(8,128)(2,1)} %bitcast.1), calls=%async_computation | async-start | bytes 1048576 | tf_op jit(solution)/shard_map/all_to_all | solution.py:50
  15.8 7.8 %all-to-all-done = bf16[8,2,128,128]{3,2,1,0:T(8,128)(2,1)S(1)} async-done(((bf16[8,2,128,128]{3,2,1,0:T(8,128)(2,1)}), bf16[8,2,128,128]{3,2,1,0:T(8,128)(2,1)S(1)}, u32[]{:S(2)}, u32[]{:S(2)}) %all-to-all-start) | async-done | bytes 524320 | tf_op jit(solution)/shard_map/all_to_all | solution.py:50
  27.5 24.3 %all-to-all-done.1 = bf16[4,128,1024]{1,2,0:T(8,128)(2,1)S(1)} async-done(((bf16[4,128,1024]{1,2,0:T(8,128)(2,1)}), bf16[4,128,1024]{1,2,0:T(8,128)(2,1)S(1)}, u32[]{:S(2)}, u32[]{:S(2)}) %all-to-all-start.1) | async-done | bytes 1048608 | tf_op jit(solution)/shard_map/all_to_all | solution.py:45
  54.9 8.0 %collective-permute-done = bf16[256,4096]{1,0:T(8,128)(2,1)} collective-permute-done((bf16[256,4096]{1,0:T(8,128)(2,1)}, bf16[256,4096]{1,0:T(8,128)(2,1)}, u32[]{:S(2)}, u32[]{:S(2)}) %collective-permute-start) | collective-permute-done | bytes 2097184 | tf_op jit(solution)/shard_map/ppermute | solution.py:12
  78.5 21.8 %all-to-all-done.2 = f32[4,128,8]{1,2,0:T(8,128)S(1)} async-done(((f32[4,128,8]{1,2,0:T(8,128)}), f32[4,128,8]{1,2,0:T(8,128)S(1)}, u32[]{:S(2)}, u32[]{:S(2)}) %all-to-all-start.2) | async-done | bytes 16416 | tf_op jit(solution)/shard_map/all_to_all | solution.py:19
  107.4 25.4 %collective-permute-done.3 = bf16[128,4096]{1,0:T(8,128)(2,1)S(1)} collective-permute-done((bf16[128,4096]{1,0:T(8,128)(2,1)S(1)}, bf16[128,4096]{1,0:T(8,128)(2,1)S(1)}, u32[]{:S(2)}, u32[]{:S(2)}) %collective-permute-start.3) | collective-permute-done | bytes 1048608 | tf_op jit(solution)/shard_map/ppermute | solution.py:12
  135.1 24.6 %collective-permute-done.4 = bf16[128,4096]{1,0:T(8,128)(2,1)S(1)} collective-permute-done((bf16[128,4096]{1,0:T(8,128)(2,1)S(1)}, bf16[128,4096]{1,0:T(8,128)(2,1)S(1)}, u32[]{:S(2)}, u32[]{:S(2)}) %collective-permute-start.4) | collective-permute-done | bytes 1048608 | tf_op jit(solution)/shard_map/ppermute | solution.py:12
  205.9 17.3 %collective-permute-done.19 = bf16[128,4096]{1,0:T(8,128)(2,1)S(1)} collective-permute-done((bf16[128,4096]{1,0:T(8,128)(2,1)S(1)}, bf16[128,4096]{1,0:T(8,128)(2,1)S(1)}, u32[]{:S(2)}, u32[]{:S(2)}) %collective-permute-start.19) | collective-permute-done | bytes 1048608 | tf_op jit(solution)/shard_map/ppermute | solution.py:12
  226.6 11.7 %collective-permute-done.50 = bf16[32,4096]{1,0:T(8,128)(2,1)S(1)} collective-permute-done((bf16[32,4096]{1,0:T(8,128)(2,1)S(1)}, bf16[32,4096]{1,0:T(8,128)(2,1)S(1)}, u32[]{:S(2)}, u32[]{:S(2)}) %collective-permute-start.50) | collective-permute-done | bytes 262176 | tf_op jit(solution)/shard_map/ppermute | solution.py:145
  240.1 8.0 %collective-permute-done.52 = bf16[32,4096]{1,0:T(8,128)(2,1)S(1)} collective-permute-done((bf16[32,4096]{1,0:T(8,128)(2,1)S(1)}, bf16[32,4096]{1,0:T(8,128)(2,1)S(1)}, u32[]{:S(2)}, u32[]{:S(2)}) %collective-permute-start.52) | collective-permute-done | bytes 262176 | tf_op jit(solution)/shard_map/ppermute | solution.py:145
  257.4 7.4 %collective-permute-done.54 = bf16[32,4096]{1,0:T(8,128)(2,1)S(1)} collective-permute-done((bf16[32,4096]{1,0:T(8,128)(2,1)S(1)}, bf16[32,4096]{1,0:T(8,128)(2,1)S(1)}, u32[]{:S(2)}, u32[]{:S(2)}) %collective-permute-start.54) | collective-permute-done | bytes 262176 | tf_op jit(solution)/shard_map/ppermute | solution.py:145
  264.9 8.5 %collective-permute-done.55 = bf16[32,4096]{1,0:T(8,128)(2,1)S(1)} collective-permute-done((bf16[32,4096]{1,0:T(8,128)(2,1)S(1)}, bf16[32,4096]{1,0:T(8,128)(2,1)S(1)}, u32[]{:S(2)}, u32[]{:S(2)}) %collective-permute-start.55) | collective-permute-done | bytes 262176 | tf_op jit(solution)/shard_map/ppermute | solution.py:145
  273.4 9.2 %collective-permute-done.56 = bf16[32,4096]{1,0:T(8,128)(2,1)S(1)} collective-permute-done((bf16[32,4096]{1,0:T(8,128)(2,1)S(1)}, bf16[32,4096]{1,0:T(8,128)(2,1)S(1)}, u32[]{:S(2)}, u32[]{:S(2)}) %collective-permute-start.56) | collective-permute-done | bytes 262176 | tf_op jit(solution)/shard_map/ppermute | solution.py:145
  289.1 7.4 %collective-permute-done.57 = bf16[32,4096]{1,0:T(8,128)(2,1)S(1)} collective-permute-done((bf16[32,4096]{1,0:T(8,128)(2,1)S(1)}, bf16[32,4096]{1,0:T(8,128)(2,1)S(1)}, u32[]{:S(2)}, u32[]{:S(2)}) %collective-permute-start.57) | collective-permute-done | bytes 262176 | tf_op jit(solution)/shard_map/ppermute | solution.py:145
  298.4 7.9 %collective-permute-done.59 = bf16[32,4096]{1,0:T(8,128)(2,1)S(1)} collective-permute-done((bf16[32,4096]{1,0:T(8,128)(2,1)S(1)}, bf16[32,4096]{1,0:T(8,128)(2,1)S(1)}, u32[]{:S(2)}, u32[]{:S(2)}) %collective-permute-start.59) | collective-permute-done | bytes 262176 | tf_op jit(solution)/shard_map/ppermute | solution.py:145
  306.4 8.6 %collective-permute-done.60 = bf16[32,4096]{1,0:T(8,128)(2,1)S(1)} collective-permute-done((bf16[32,4096]{1,0:T(8,128)(2,1)S(1)}, bf16[32,4096]{1,0:T(8,128)(2,1)S(1)}, u32[]{:S(2)}, u32[]{:S(2)}) %collective-permute-start.60) | collective-permute-done | bytes 262176 | tf_op jit(solution)/shard_map/ppermute | solution.py:145
  315.9 7.9 %collective-permute-done.61 = bf16[32,4096]{1,0:T(8,128)(2,1)S(1)} collective-permute-done((bf16[32,4096]{1,0:T(8,128)(2,1)S(1)}, bf16[32,4096]{1,0:T(8,128)(2,1)S(1)}, u32[]{:S(2)}, u32[]{:S(2)}) %collective-permute-start.61) | collective-permute-done | bytes 262176 | tf_op jit(solution)/shard_map/ppermute | solution.py:145
  323.8 7.6 %collective-permute-done.62 = bf16[32,4096]{1,0:T(8,128)(2,1)S(1)} collective-permute-done((bf16[32,4096]{1,0:T(8,128)(2,1)S(1)}, bf16[32,4096]{1,0:T(8,128)(2,1)S(1)}, u32[]{:S(2)}, u32[]{:S(2)}) %collective-permute-start.62) | collective-permute-done | bytes 262176 | tf_op jit(solution)/shard_map/ppermute | solution.py:145
  356.8 7.4 %collective-permute-done.40 = bf16[32,4096]{1,0:T(8,128)(2,1)S(1)} collective-permute-done((bf16[32,4096]{1,0:T(8,128)(2,1)S(1)}, bf16[32,4096]{1,0:T(8,128)(2,1)S(1)}, u32[]{:S(2)}, u32[]{:S(2)}) %collective-permute-start.40) | collective-permute-done | bytes 262176 | tf_op jit(solution)/shard_map/ppermute | solution.py:145
  391.1 7.2 %collective-permute-done.45 = bf16[32,4096]{1,0:T(8,128)(2,1)S(1)} collective-permute-done((bf16[32,4096]{1,0:T(8,128)(2,1)S(1)}, bf16[32,4096]{1,0:T(8,128)(2,1)S(1)}, u32[]{:S(2)}, u32[]{:S(2)}) %collective-permute-start.45) | collective-permute-done | bytes 262176 | tf_op jit(solution)/shard_map/ppermute | solution.py:145
  416.2 8.5 %collective-permute-done.48 = bf16[32,4096]{1,0:T(8,128)(2,1)S(1)} collective-permute-done((bf16[32,4096]{1,0:T(8,128)(2,1)S(1)}, bf16[32,4096]{1,0:T(8,128)(2,1)S(1)}, u32[]{:S(2)}, u32[]{:S(2)}) %collective-permute-start.48) | collective-permute-done | bytes 262176 | tf_op jit(solution)/shard_map/ppermute | solution.py:145
  426.0 8.3 %collective-permute-done.49 = bf16[32,4096]{1,0:T(8,128)(2,1)S(1)} collective-permute-done((bf16[32,4096]{1,0:T(8,128)(2,1)S(1)}, bf16[32,4096]{1,0:T(8,128)(2,1)S(1)}, u32[]{:S(2)}, u32[]{:S(2)}) %collective-permute-start.49) | collective-permute-done | bytes 262176 | tf_op jit(solution)/shard_map/ppermute | solution.py:145
  435.3 7.6 %collective-permute-done.22 = bf16[32,4096]{1,0:T(8,128)(2,1)S(1)} collective-permute-done((bf16[32,4096]{1,0:T(8,128)(2,1)S(1)}, bf16[32,4096]{1,0:T(8,128)(2,1)S(1)}, u32[]{:S(2)}, u32[]{:S(2)}) %collective-permute-start.22) | collective-permute-done | bytes 262176 | tf_op jit(solution)/shard_map/ppermute | solution.py:145
  445.2 7.5 %collective-permute-done.24 = bf16[32,4096]{1,0:T(8,128)(2,1)S(1)} collective-permute-done((bf16[32,4096]{1,0:T(8,128)(2,1)S(1)}, bf16[32,4096]{1,0:T(8,128)(2,1)S(1)}, u32[]{:S(2)}, u32[]{:S(2)}) %collective-permute-start.24) | collective-permute-done | bytes 262176 | tf_op jit(solution)/shard_map/ppermute | solution.py:145
  452.8 8.3 %collective-permute-done.25 = bf16[32,4096]{1,0:T(8,128)(2,1)S(1)} collective-permute-done((bf16[32,4096]{1,0:T(8,128)(2,1)S(1)}, bf16[32,4096]{1,0:T(8,128)(2,1)S(1)}, u32[]{:S(2)}, u32[]{:S(2)}) %collective-permute-start.25) | collective-permute-done | bytes 262176 | tf_op jit(solution)/shard_map/ppermute | solution.py:145
  461.8 7.7 %collective-permute-done.26 = bf16[32,4096]{1,0:T(8,128)(2,1)S(1)} collective-permute-done((bf16[32,4096]{1,0:T(8,128)(2,1)S(1)}, bf16[32,4096]{1,0:T(8,128)(2,1)S(1)}, u32[]{:S(2)}, u32[]{:S(2)}) %collective-permute-start.26) | collective-permute-done | bytes 262176 | tf_op jit(solution)/shard_map/ppermute | solution.py:145
  469.5 7.7 %collective-permute-done.27 = bf16[32,4096]{1,0:T(8,128)(2,1)S(1)} collective-permute-done((bf16[32,4096]{1,0:T(8,128)(2,1)S(1)}, bf16[32,4096]{1,0:T(8,128)(2,1)S(1)}, u32[]{:S(2)}, u32[]{:S(2)}) %collective-permute-start.27) | collective-permute-done | bytes 262176 | tf_op jit(solution)/shard_map/ppermute | solution.py:145
  478.9 7.4 %collective-permute-done.28 = bf16[32,4096]{1,0:T(8,128)(2,1)S(1)} collective-permute-done((bf16[32,4096]{1,0:T(8,128)(2,1)S(1)}, bf16[32,4096]{1,0:T(8,128)(2,1)S(1)}, u32[]{:S(2)}, u32[]{:S(2)}) %collective-permute-start.28) | collective-permute-done | bytes 262176 | tf_op jit(solution)/shard_map/ppermute | solution.py:145
  502.1 7.5 %collective-permute-done.31 = bf16[32,4096]{1,0:T(8,128)(2,1)S(1)} collective-permute-done((bf16[32,4096]{1,0:T(8,128)(2,1)S(1)}, bf16[32,4096]{1,0:T(8,128)(2,1)S(1)}, u32[]{:S(2)}, u32[]{:S(2)}) %collective-permute-start.31) | collective-permute-done | bytes 262176 | tf_op jit(solution)/shard_map/ppermute | solution.py:145
  527.5 8.5 %collective-permute-done.34 = bf16[32,4096]{1,0:T(8,128)(2,1)S(1)} collective-permute-done((bf16[32,4096]{1,0:T(8,128)(2,1)S(1)}, bf16[32,4096]{1,0:T(8,128)(2,1)S(1)}, u32[]{:S(2)}, u32[]{:S(2)}) %collective-permute-start.34) | collective-permute-done | bytes 262176 | tf_op jit(solution)/shard_map/ppermute | solution.py:145
  536.0 9.2 %collective-permute-done.35 = bf16[32,4096]{1,0:T(8,128)(2,1)S(1)} collective-permute-done((bf16[32,4096]{1,0:T(8,128)(2,1)S(1)}, bf16[32,4096]{1,0:T(8,128)(2,1)S(1)}, u32[]{:S(2)}, u32[]{:S(2)}) %collective-permute-start.35) | collective-permute-done | bytes 262176 | tf_op jit(solution)/shard_map/ppermute | solution.py:145
  545.9 27.1 %collective-permute-done.66 = bf16[128,4096]{1,0:T(8,128)(2,1)S(1)} collective-permute-done((bf16[128,4096]{1,0:T(8,128)(2,1)S(1)}, bf16[128,4096]{1,0:T(8,128)(2,1)S(1)}, u32[]{:S(2)}, u32[]{:S(2)}) %collective-permute-start.66) | collective-permute-done | bytes 1048608 | tf_op jit(solution)/shard_map/ppermute | solution.py:12
  (278 shorter events, 222.7 us)
Async XLA Ops:
  1.9 21.8 %all-to-all-start = ((bf16[8,2,128,128]{3,2,1,0:T(8,128)(2,1)}), bf16[8,2,128,128]{3,2,1,0:T(8,128)(2,1)S(1)}, u32[]{:S(2)}, u32[]{:S(2)}) async-start(bf16[8,2,128,128]{3,2,1,0:T(8,128)(2,1)} %bitcast.1), calls=%async_computation | async-start | bytes 1048576 | tf_op jit(solution)/shard_map/all_to_all | solution.py:50
  12.4 50.5 %collective-permute-start = (bf16[256,4096]{1,0:T(8,128)(2,1)}, bf16[256,4096]{1,0:T(8,128)(2,1)}, u32[]{:S(2)}, u32[]{:S(2)}) collective-permute-start(bf16[256,4096]{1,0:T(8,128)(2,1)} %constant_dynamic-slice_fusion), channel_id=1, source_target_pairs={{0,1},{1,0},{2,3},{3,2},{4,5},{5,4},{6,7},{7,6},{8,9},{9,8},{10,11... | collective-permute-start | bytes 6291464 | tf_op jit(solution)/shard_map/ppermute | solution.py:12
  23.7 28.2 %all-to-all-start.1 = ((bf16[4,128,1024]{1,2,0:T(8,128)(2,1)}), bf16[4,128,1024]{1,2,0:T(8,128)(2,1)S(1)}, u32[]{:S(2)}, u32[]{:S(2)}) async-start(bf16[4,128,1024]{1,2,0:T(8,128)(2,1)} %bitcast.5), calls=%async_computation.1 | async-start | bytes 2097152 | tf_op jit(solution)/shard_map/all_to_all | solution.py:45
  72.3 31.0 %collective-permute-start.2 = (bf16[128,4096]{1,0:T(8,128)(2,1)}, bf16[128,4096]{1,0:T(8,128)(2,1)}, u32[]{:S(2)}, u32[]{:S(2)}) collective-permute-start(bf16[128,4096]{1,0:T(8,128)(2,1)} %fusion.35), channel_id=1, source_target_pairs={{0,2},{2,4},{4,6},{6,0},{1,3},{3,5},{5,7},{7,1},{8,10},{10,12},{12... | collective-permute-start | bytes 3145736 | tf_op jit(solution)/shard_map/ppermute | solution.py:12
  75.1 25.2 %all-to-all-start.2 = ((f32[4,128,8]{1,2,0:T(8,128)}), f32[4,128,8]{1,2,0:T(8,128)S(1)}, u32[]{:S(2)}, u32[]{:S(2)}) async-start(f32[4,128,8]{1,2,0:T(8,128)} %broadcast_in_dim.189), calls=%async_computation.2 | async-start | bytes 32768 | tf_op jit(solution)/shard_map/all_to_all | solution.py:19
  105.7 27.1 %collective-permute-start.3 = (bf16[128,4096]{1,0:T(8,128)(2,1)S(1)}, bf16[128,4096]{1,0:T(8,128)(2,1)S(1)}, u32[]{:S(2)}, u32[]{:S(2)}) collective-permute-start(bf16[128,4096]{1,0:T(8,128)(2,1)S(1)} %fusion.34), channel_id=1, source_target_pairs={{0,2},{2,4},{4,6},{6,0},{1,3},{3,5},{5,7},{7,1},{8,10},{10,12},{12... | collective-permute-start | bytes 3145736 | tf_op jit(solution)/shard_map/ppermute | solution.py:12
  133.7 26.1 %collective-permute-start.4 = (bf16[128,4096]{1,0:T(8,128)(2,1)S(1)}, bf16[128,4096]{1,0:T(8,128)(2,1)S(1)}, u32[]{:S(2)}, u32[]{:S(2)}) collective-permute-start(bf16[128,4096]{1,0:T(8,128)(2,1)S(1)} %fusion.33), channel_id=1, source_target_pairs={{0,2},{2,4},{4,6},{6,0},{1,3},{3,5},{5,7},{7,1},{8,10},{10,12},{12... | collective-permute-start | bytes 3145736 | tf_op jit(solution)/shard_map/ppermute | solution.py:12
  162.2 9.3 %collective-permute-start.5 = (bf16[32,4096]{1,0:T(8,128)(2,1)S(1)}, bf16[32,4096]{1,0:T(8,128)(2,1)S(1)}, u32[]{:S(2)}, u32[]{:S(2)}) collective-permute-start(bf16[32,4096]{1,0:T(8,128)(2,1)S(1)} %get-tuple-element.77), channel_id=1, source_target_pairs={{0,1},{1,0},{8,9},{9,8},{16,17},{17,16},{24,25},{25,24},{2,3},{3,2... | collective-permute-start | bytes 786440 | tf_op jit(solution)/shard_map/ppermute | solution.py:145
  162.4 14.8 %collective-permute-start.7 = (bf16[32,4096]{1,0:T(8,128)(2,1)S(1)}, bf16[32,4096]{1,0:T(8,128)(2,1)S(1)}, u32[]{:S(2)}, u32[]{:S(2)}) collective-permute-start(bf16[32,4096]{1,0:T(8,128)(2,1)S(1)} %get-tuple-element.75), channel_id=1, source_target_pairs={{0,9},{1,8},{8,1},{9,0},{16,25},{17,24},{24,17},{25,16},{2,11},{3,... | collective-permute-start | bytes 786440 | tf_op jit(solution)/shard_map/ppermute | solution.py:145
  164.5 12.8 %collective-permute-start.8 = (bf16[32,4096]{1,0:T(8,128)(2,1)S(1)}, bf16[32,4096]{1,0:T(8,128)(2,1)S(1)}, u32[]{:S(2)}, u32[]{:S(2)}) collective-permute-start(bf16[32,4096]{1,0:T(8,128)(2,1)S(1)} %get-tuple-element.74), channel_id=1, source_target_pairs={{0,16},{1,17},{8,24},{9,25},{16,0},{17,1},{24,8},{25,9},{2,18},{3,... | collective-permute-start | bytes 786440 | tf_op jit(solution)/shard_map/ppermute | solution.py:145
  166.0 12.8 %collective-permute-start.9 = (bf16[32,4096]{1,0:T(8,128)(2,1)S(1)}, bf16[32,4096]{1,0:T(8,128)(2,1)S(1)}, u32[]{:S(2)}, u32[]{:S(2)}) collective-permute-start(bf16[32,4096]{1,0:T(8,128)(2,1)S(1)} %get-tuple-element.73), channel_id=1, source_target_pairs={{0,17},{1,16},{8,25},{9,24},{16,1},{17,0},{24,9},{25,8},{2,19},{3,... | collective-permute-start | bytes 786440 | tf_op jit(solution)/shard_map/ppermute | solution.py:145
  171.6 12.4 %collective-permute-start.10 = (bf16[32,4096]{1,0:T(8,128)(2,1)S(1)}, bf16[32,4096]{1,0:T(8,128)(2,1)S(1)}, u32[]{:S(2)}, u32[]{:S(2)}) collective-permute-start(bf16[32,4096]{1,0:T(8,128)(2,1)S(1)} %get-tuple-element.72), channel_id=1, source_target_pairs={{0,24},{1,25},{8,16},{9,17},{16,8},{17,9},{24,0},{25,1},{2,26},{3,... | collective-permute-start | bytes 786440 | tf_op jit(solution)/shard_map/ppermute | solution.py:145
  171.6 17.2 %collective-permute-start.11 = (bf16[32,4096]{1,0:T(8,128)(2,1)S(1)}, bf16[32,4096]{1,0:T(8,128)(2,1)S(1)}, u32[]{:S(2)}, u32[]{:S(2)}) collective-permute-start(bf16[32,4096]{1,0:T(8,128)(2,1)S(1)} %get-tuple-element.71), channel_id=1, source_target_pairs={{0,25},{1,24},{8,17},{9,16},{16,9},{17,8},{24,1},{25,0},{2,27},{3,... | collective-permute-start | bytes 786440 | tf_op jit(solution)/shard_map/ppermute | solution.py:145
  195.7 27.6 %collective-permute-start.19 = (bf16[128,4096]{1,0:T(8,128)(2,1)S(1)}, bf16[128,4096]{1,0:T(8,128)(2,1)S(1)}, u32[]{:S(2)}, u32[]{:S(2)}) collective-permute-start(bf16[128,4096]{1,0:T(8,128)(2,1)S(1)} %multiply_convert_fusion), channel_id=1, source_target_pairs={{0,2},{2,4},{4,6},{6,0},{1,3},{3,5},{5,7},{7,1},{8,10},{10,12},{12... | collective-permute-start | bytes 3145736 | tf_op jit(solution)/shard_map/ppermute | solution.py:12
  196.2 9.7 %collective-permute-start.13 = (bf16[32,4096]{1,0:T(8,128)(2,1)S(1)}, bf16[32,4096]{1,0:T(8,128)(2,1)S(1)}, u32[]{:S(2)}, u32[]{:S(2)}) collective-permute-start(bf16[32,4096]{1,0:T(8,128)(2,1)S(1)} %get-tuple-element.68), channel_id=1, source_target_pairs={{0,8},{1,9},{8,0},{9,1},{16,24},{17,25},{24,16},{25,17},{2,10},{3,... | collective-permute-start | bytes 786440 | tf_op jit(solution)/shard_map/ppermute | solution.py:145
  196.7 27.7 %collective-permute-start.14 = (bf16[32,4096]{1,0:T(8,128)(2,1)S(1)}, bf16[32,4096]{1,0:T(8,128)(2,1)S(1)}, u32[]{:S(2)}, u32[]{:S(2)}) collective-permute-start(bf16[32,4096]{1,0:T(8,128)(2,1)S(1)} %get-tuple-element.67), channel_id=1, source_target_pairs={{0,9},{1,8},{8,1},{9,0},{16,25},{17,24},{24,17},{25,16},{2,11},{3,... | collective-permute-start | bytes 786440 | tf_op jit(solution)/shard_map/ppermute | solution.py:145
  197.1 91.7 %collective-permute-start.15 = (bf16[32,4096]{1,0:T(8,128)(2,1)S(1)}, bf16[32,4096]{1,0:T(8,128)(2,1)S(1)}, u32[]{:S(2)}, u32[]{:S(2)}) collective-permute-start(bf16[32,4096]{1,0:T(8,128)(2,1)S(1)} %get-tuple-element.66), channel_id=1, source_target_pairs={{0,16},{1,17},{8,24},{9,25},{16,0},{17,1},{24,8},{25,9},{2,18},{3,... | collective-permute-start | bytes 786440 | tf_op jit(solution)/shard_map/ppermute | solution.py:145
  203.5 342.3 %collective-permute-start.16 = (bf16[32,4096]{1,0:T(8,128)(2,1)S(1)}, bf16[32,4096]{1,0:T(8,128)(2,1)S(1)}, u32[]{:S(2)}, u32[]{:S(2)}) collective-permute-start(bf16[32,4096]{1,0:T(8,128)(2,1)S(1)} %get-tuple-element.65), channel_id=1, source_target_pairs={{0,17},{1,16},{8,25},{9,24},{16,1},{17,0},{24,9},{25,8},{2,19},{3,... | collective-permute-start | bytes 786440 | tf_op jit(solution)/shard_map/ppermute | solution.py:145
  205.8 340.0 %collective-permute-start.17 = (bf16[32,4096]{1,0:T(8,128)(2,1)S(1)}, bf16[32,4096]{1,0:T(8,128)(2,1)S(1)}, u32[]{:S(2)}, u32[]{:S(2)}) collective-permute-start(bf16[32,4096]{1,0:T(8,128)(2,1)S(1)} %get-tuple-element.64), channel_id=1, source_target_pairs={{0,24},{1,25},{8,16},{9,17},{16,8},{17,9},{24,0},{25,1},{2,26},{3,... | collective-permute-start | bytes 786440 | tf_op jit(solution)/shard_map/ppermute | solution.py:145
  223.2 322.6 %collective-permute-start.18 = (bf16[32,4096]{1,0:T(8,128)(2,1)S(1)}, bf16[32,4096]{1,0:T(8,128)(2,1)S(1)}, u32[]{:S(2)}, u32[]{:S(2)}) collective-permute-start(bf16[32,4096]{1,0:T(8,128)(2,1)S(1)} %get-tuple-element.63), channel_id=1, source_target_pairs={{0,25},{1,24},{8,17},{9,16},{16,9},{17,8},{24,1},{25,0},{2,27},{3,... | collective-permute-start | bytes 786440 | tf_op jit(solution)/shard_map/ppermute | solution.py:145
  224.4 13.8 %collective-permute-start.50 = (bf16[32,4096]{1,0:T(8,128)(2,1)S(1)}, bf16[32,4096]{1,0:T(8,128)(2,1)S(1)}, u32[]{:S(2)}, u32[]{:S(2)}) collective-permute-start(bf16[32,4096]{1,0:T(8,128)(2,1)S(1)} %get-tuple-element.29), channel_id=1, source_target_pairs={{0,1},{1,0},{8,9},{9,8},{16,17},{17,16},{24,25},{25,24},{2,3},{3,2... | collective-permute-start | bytes 786440 | tf_op jit(solution)/shard_map/ppermute | solution.py:145
  288.8 43.7 %collective-permute-start.20 = (bf16[128,4096]{1,0:T(8,128)(2,1)S(1)}, bf16[128,4096]{1,0:T(8,128)(2,1)S(1)}, u32[]{:S(2)}, u32[]{:S(2)}) collective-permute-start(bf16[128,4096]{1,0:T(8,128)(2,1)S(1)} %collective-permute-done.19), channel_id=1, source_target_pairs={{0,2},{2,4},{4,6},{6,0},{1,3},{3,5},{5,7},{7,1},{8,10},{10,12},{12... | collective-permute-start | bytes 3145736 | tf_op jit(solution)/shard_map/ppermute | solution.py:12
  333.4 12.4 %collective-permute-start.36 = (bf16[32,4096]{1,0:T(8,128)(2,1)S(1)}, bf16[32,4096]{1,0:T(8,128)(2,1)S(1)}, u32[]{:S(2)}, u32[]{:S(2)}) collective-permute-start(bf16[32,4096]{1,0:T(8,128)(2,1)S(1)} %get-tuple-element.45), channel_id=1, source_target_pairs={{0,1},{1,0},{8,9},{9,8},{16,17},{17,16},{24,25},{25,24},{2,3},{3,2... | collective-permute-start | bytes 786440 | tf_op jit(solution)/shard_map/ppermute | solution.py:145
  346.9 9.5 %collective-permute-start.39 = (bf16[32,4096]{1,0:T(8,128)(2,1)S(1)}, bf16[32,4096]{1,0:T(8,128)(2,1)S(1)}, u32[]{:S(2)}, u32[]{:S(2)}) collective-permute-start(bf16[32,4096]{1,0:T(8,128)(2,1)S(1)} %get-tuple-element.42), channel_id=1, source_target_pairs={{0,16},{1,17},{8,24},{9,25},{16,0},{17,1},{24,8},{25,9},{2,18},{3,... | collective-permute-start | bytes 786440 | tf_op jit(solution)/shard_map/ppermute | solution.py:145
  354.2 10.0 %collective-permute-start.40 = (bf16[32,4096]{1,0:T(8,128)(2,1)S(1)}, bf16[32,4096]{1,0:T(8,128)(2,1)S(1)}, u32[]{:S(2)}, u32[]{:S(2)}) collective-permute-start(bf16[32,4096]{1,0:T(8,128)(2,1)S(1)} %get-tuple-element.41), channel_id=1, source_target_pairs={{0,17},{1,16},{8,25},{9,24},{16,1},{17,0},{24,9},{25,8},{2,19},{3,... | collective-permute-start | bytes 786440 | tf_op jit(solution)/shard_map/ppermute | solution.py:145
  356.4 12.2 %collective-permute-start.41 = (bf16[32,4096]{1,0:T(8,128)(2,1)S(1)}, bf16[32,4096]{1,0:T(8,128)(2,1)S(1)}, u32[]{:S(2)}, u32[]{:S(2)}) collective-permute-start(bf16[32,4096]{1,0:T(8,128)(2,1)S(1)} %get-tuple-element.40), channel_id=1, source_target_pairs={{0,24},{1,25},{8,16},{9,17},{16,8},{17,9},{24,0},{25,1},{2,26},{3,... | collective-permute-start | bytes 786440 | tf_op jit(solution)/shard_map/ppermute | solution.py:145
  364.2 10.1 %collective-permute-start.42 = (bf16[32,4096]{1,0:T(8,128)(2,1)S(1)}, bf16[32,4096]{1,0:T(8,128)(2,1)S(1)}, u32[]{:S(2)}, u32[]{:S(2)}) collective-permute-start(bf16[32,4096]{1,0:T(8,128)(2,1)S(1)} %get-tuple-element.39), channel_id=1, source_target_pairs={{0,25},{1,24},{8,17},{9,16},{16,9},{17,8},{24,1},{25,0},{2,27},{3,... | collective-permute-start | bytes 786440 | tf_op jit(solution)/shard_map/ppermute | solution.py:145
  381.7 43.3 %collective-permute-start.21 = (bf16[128,4096]{1,0:T(8,128)(2,1)S(1)}, bf16[128,4096]{1,0:T(8,128)(2,1)S(1)}, u32[]{:S(2)}, u32[]{:S(2)}) collective-permute-start(bf16[128,4096]{1,0:T(8,128)(2,1)S(1)} %collective-permute-done.20), channel_id=1, source_target_pairs={{0,2},{2,4},{4,6},{6,0},{1,3},{3,5},{5,7},{7,1},{8,10},{10,12},{12... | collective-permute-start | bytes 3145736 | tf_op jit(solution)/shard_map/ppermute | solution.py:12
  424.7 68.2 %collective-permute-start.64 = (bf16[128,4096]{1,0:T(8,128)(2,1)S(1)}, bf16[128,4096]{1,0:T(8,128)(2,1)S(1)}, u32[]{:S(2)}, u32[]{:S(2)}) collective-permute-start(bf16[128,4096]{1,0:T(8,128)(2,1)S(1)} %convolution_convert_fusion.4), channel_id=1, source_target_pairs={{0,2},{2,4},{4,6},{6,0},{1,3},{3,5},{5,7},{7,1},{8,10},{10,12},{12... | collective-permute-start | bytes 3145736 | tf_op jit(solution)/shard_map/ppermute | solution.py:12
  425.0 9.3 %collective-permute-start.49 = (bf16[32,4096]{1,0:T(8,128)(2,1)S(1)}, bf16[32,4096]{1,0:T(8,128)(2,1)S(1)}, u32[]{:S(2)}, u32[]{:S(2)}) collective-permute-start(bf16[32,4096]{1,0:T(8,128)(2,1)S(1)} %get-tuple-element.31), channel_id=1, source_target_pairs={{0,25},{1,24},{8,17},{9,16},{16,9},{17,8},{24,1},{25,0},{2,27},{3,... | collective-permute-start | bytes 786440 | tf_op jit(solution)/shard_map/ppermute | solution.py:145
  493.4 51.9 %collective-permute-start.65 = (bf16[128,4096]{1,0:T(8,128)(2,1)S(1)}, bf16[128,4096]{1,0:T(8,128)(2,1)S(1)}, u32[]{:S(2)}, u32[]{:S(2)}) collective-permute-start(bf16[128,4096]{1,0:T(8,128)(2,1)S(1)} %fusion.38), channel_id=1, source_target_pairs={{0,2},{2,4},{4,6},{6,0},{1,3},{3,5},{5,7},{7,1},{8,10},{10,12},{12... | collective-permute-start | bytes 3145736 | tf_op jit(solution)/shard_map/ppermute | solution.py:12
  545.7 27.3 %collective-permute-start.66 = (bf16[128,4096]{1,0:T(8,128)(2,1)S(1)}, bf16[128,4096]{1,0:T(8,128)(2,1)S(1)}, u32[]{:S(2)}, u32[]{:S(2)}) collective-permute-start(bf16[128,4096]{1,0:T(8,128)(2,1)S(1)} %fusion.37), channel_id=1, source_target_pairs={{0,2},{2,4},{4,6},{6,0},{1,3},{3,5},{5,7},{7,1},{8,10},{10,12},{12... | collective-permute-start | bytes 3145736 | tf_op jit(solution)/shard_map/ppermute | solution.py:12
  (52 other events, 446.5 us)
